TPU v7x, 32 devices: a whole 2x2x4 slice. The times are simulated.
32 devices in a mesh: grp: 2 (over y), seq: 4 (over z), var: 2 (over x), rep: 2 (over core).
Axes of the slice: x: 2, y: 2, z: 4, core: 2. Of those that a mesh axis runs over, the one named last changes fastest.
Arguments:
- cache_vals: bfloat16 [256, 8, 1536], P(('grp', 'seq', 'var')), parts along dimension 0, may hold values from -6 to 6
- cache_scales: bfloat16 [256, 1536], P(('grp', 'seq', 'var')), parts along dimension 0, may hold values from 0.29882812 to 3
- block_slot: int32 [256], P('grp'), parts along dimension 0, may hold values from 0 to 127, as said below
- block_lists: int32 [256, 4], P(('grp', 'seq', 'var')), parts along dimension 0, may hold values from 0 to 127, as said below
- variant_pos: int32 [256], P(('grp', 'seq', 'var')), parts along dimension 0, may hold values from 0 to 1008, as said below
- window_offsets: int32 [256], P(('grp', 'seq', 'var')), parts along dimension 0, may hold values from 0 to 15
- variant_deltas: bfloat16 [256, 1536], P(('grp', 'seq', 'var')), parts along dimension 0, may hold values from -12 to 12
- conv_taps: bfloat16 [17, 1536], replicated, may hold values from -1.5 to 1.5
- norm_gain: float32 [1536], replicated, may hold values from 0.1 to 1.9
- w_query: bfloat16 [1536, 512], P(None, 'rep'), may hold values from -0.15625 to 0.15625
- w_key: bfloat16 [1536, 512], P(None, 'rep'), may hold values from -0.3359375 to 0.3359375
- w_value: bfloat16 [1536, 768], P(None, 'rep'), may hold values from -0.609375 to 0.609375
- ref_keys: bfloat16 [2048, 512], P(('grp', 'seq'), 'rep'), parts along dimension 0, may hold values from -200 to 200
- ref_values: bfloat16 [2048, 768], P(('grp', 'seq'), 'rep'), parts along dimension 0, may hold values from -24 to 24
- head_slopes: float32 [4], P('rep'), may hold values from 3e-05 to 0.03
Outputs:
- variant_out: bfloat16 [256, 16, 768], P(('grp', 'seq', 'var'), None, 'rep'), parts along dimension 0
There are 2 independent parts, one for each index of `grp`. A program takes and returns all parts, laid end to end along the dimension named above; an argument that names none is the same for every part. Nothing has to cross between parts.
Inputs may be any that keep to these rules, and one draw needn't show every extreme that they name: `block_slot`: each of 0 .. 127 once. block_lists[v] = a - 1, a, a + 1, a + 2 with a = variant_pos[v] / 8, the blocks around the variant's recomputed rows. Among the rows of one device along seq and var, the entries at even positions k name at most 8 blocks whose slot lies on any one device (slot // 16 along seq and var), and likewise the entries at odd k; in every draw some device reads exactly 8 entries of each parity, 16 in all, from one and the same device. `variant_pos`: a multiple of 8.
All inputs are finite; a program needn't handle non-finite values.
Results may differ from a plain program's by a relative error of at most 0.0095.
The roundings to bfloat16 on the way count: a program that leaves them out, or rounds other values in their place, can miss the bound.
Values may be sent and summed in bfloat16 or wider, within the bound.
No kernel may reach another device: no remote copies, remote signals or barrier semaphores. Data moves between devices by JAX's collectives and lax.ppermute only.
A program may use at most 64 MiB of HBM per device.

v0:
```python
import math

import jax
import jax.numpy as jnp
from jax import lax
from jax.sharding import PartitionSpec as P

W = 16
RADIUS = 8


EPSILON = 1e-06


def entry_ranks(slot_ids, per_owner):
    owner_ids = slot_ids // per_owner
    local_ids = slot_ids % per_owner
    position = jnp.arange(slot_ids.shape[0], dtype=jnp.int32)
    earlier = (owner_ids[:, None] == owner_ids[None, :]) & (position[None, :] < position[:, None])
    return (owner_ids, local_ids, jnp.sum(earlier.astype(jnp.int32), axis=1))


def request_table(owner_ids, local_ids, rank_ids, owners, capacity):
    owner_axis = jnp.arange(owners, dtype=jnp.int32)
    slot_axis = jnp.arange(capacity, dtype=jnp.int32)
    matched = (owner_ids[:, None, None] == owner_axis[None, :, None]) & (
        rank_ids[:, None, None] == slot_axis[None, None, :]
    )
    return jnp.sum(jnp.where(matched, local_ids[:, None, None] + 1, 0), axis=0) - 1


def on_device(
    cache_vals,
    cache_scales,
    block_slot,
    block_lists,
    variant_pos,
    window_offsets,
    variant_deltas,
    conv_taps,
    norm_gain,
    w_query,
    w_key,
    w_value,
    ref_keys,
    ref_values,
    head_slopes,
):
    owners = lax.axis_size(("seq", "var"))
    per_owner = cache_vals.shape[0]
    block_rows = cache_vals.shape[1]
    channels = cache_vals.shape[2]
    variants, per_variant = block_lists.shape
    base_capacity = (variants * per_variant + owners - 1) // owners
    columns = 2 * jnp.arange(per_variant // 2, dtype=jnp.int32) + lax.axis_index("rep")
    columns_taken = columns.shape[0]
    my_slots = jnp.take(block_slot, jnp.take(block_lists, columns, axis=1), axis=0).reshape(-1)
    owner_ids, local_ids, rank_ids = entry_ranks(my_slots, per_owner)
    request_rows = request_table(owner_ids, local_ids, rank_ids, owners, base_capacity)
    wanted = lax.all_to_all(request_rows, ("seq", "var"), split_axis=0, concat_axis=0, tiled=True)
    present = wanted >= 0
    chosen = jnp.clip(wanted, 0, per_owner - 1)
    send_blocks = jnp.where(
        present[:, :, None, None], jnp.take(cache_vals, chosen, axis=0), jnp.zeros((), jnp.bfloat16)
    )
    send_scales = jnp.where(
        present[:, :, None], jnp.take(cache_scales, chosen, axis=0), jnp.zeros((), jnp.bfloat16)
    )
    got_blocks, got_scales = (
        lax.all_to_all(send_blocks, ("seq", "var"), split_axis=0, concat_axis=0, tiled=True),
        lax.all_to_all(send_scales, ("seq", "var"), split_axis=0, concat_axis=0, tiled=True),
    )
    arrival = owner_ids * base_capacity + rank_ids
    fetched = jnp.take(
        got_blocks.reshape(owners * base_capacity, block_rows, channels), arrival, axis=0
    )
    fetched_scales = jnp.take(got_scales.reshape(owners * base_capacity, channels), arrival, axis=0)
    fetched, fetched_scales = (
        lax.all_gather(
            fetched.reshape(variants, columns_taken, 1, block_rows, channels),
            "rep",
            axis=2,
            tiled=True,
        ),
        lax.all_gather(
            fetched_scales.reshape(variants, columns_taken, 1, channels), "rep", axis=2, tiled=True
        ),
    )
    fetched = fetched.reshape(variants, per_variant, block_rows, channels)
    fetched_scales = fetched_scales.reshape(variants, per_variant, channels)
    context = (
        fetched.astype(jnp.float32) * fetched_scales.astype(jnp.float32)[:, :, None, :]
    ).reshape(variants, per_variant * block_rows, channels)
    rows_context = per_variant * block_rows
    marker = (
        jnp.arange(rows_context, dtype=jnp.int32)[None, :] == (RADIUS + window_offsets)[:, None]
    ).astype(jnp.float32)
    altered = context + marker[:, :, None] * variant_deltas.astype(jnp.float32)[:, None, :]
    tap_table = conv_taps.astype(jnp.float32)
    tower_rows = altered[:, RADIUS : RADIUS + W]
    for tap_index in range(2 * RADIUS + 1):
        tower_rows = tower_rows + tap_table[tap_index] * altered[:, tap_index : tap_index + W]
    mean_square = jnp.mean(tower_rows * tower_rows, axis=-1, keepdims=True)
    normed = (tower_rows * lax.rsqrt(mean_square + EPSILON) * norm_gain).astype(jnp.bfloat16)
    local_heads = head_slopes.shape[0]
    key_width = w_query.shape[1] // local_heads
    value_width = w_value.shape[1] // local_heads
    inverse_root = 1.0 / math.sqrt(key_width)
    flat_rows = normed.reshape(variants * W, channels)
    queries = jnp.dot(flat_rows, w_query, preferred_element_type=jnp.float32).astype(jnp.bfloat16)
    own_keys = jnp.dot(flat_rows, w_key, preferred_element_type=jnp.float32).astype(jnp.bfloat16)
    own_values = jnp.dot(flat_rows, w_value, preferred_element_type=jnp.float32).astype(
        jnp.bfloat16
    )
    query_heads = queries.reshape(variants, W, local_heads, key_width)
    own_key_heads = own_keys.reshape(variants, W, local_heads, key_width)
    own_value_heads = own_values.reshape(variants, W, local_heads, value_width)
    row_offsets = jnp.arange(W, dtype=jnp.int32)
    near_distance = jnp.abs(row_offsets[:, None] - row_offsets[None, :]).astype(jnp.float32)
    near_scores = (
        jnp.einsum(
            "vthd,vshd->vths", query_heads, own_key_heads, preferred_element_type=jnp.float32
        )
        * inverse_root
        - head_slopes[None, None, :, None] * near_distance[None, :, None, :]
    )
    near_peak = jnp.max(near_scores, axis=-1)
    near_exp = jnp.exp(near_scores - near_peak[..., None])
    near_total = jnp.sum(near_exp, axis=-1)
    near_sum = jnp.einsum(
        "vths,vshd->vthd",
        near_exp.astype(jnp.bfloat16),
        own_value_heads,
        preferred_element_type=jnp.float32,
    )
    rows_total = variants * W
    initial = (
        near_peak.reshape(rows_total, local_heads),
        near_total.reshape(rows_total, local_heads),
        near_sum.reshape(rows_total, local_heads, value_width),
    )
    query_flat = query_heads.reshape(rows_total, local_heads, key_width)
    query_pos = (variant_pos[:, None] + row_offsets[None, :]).reshape(-1)
    query_start = jnp.repeat(variant_pos, W)

    def absorb(state_in, key_block, value_block, first_key):
        best_score, running_total, running_sum = state_in
        count_keys = key_block.shape[0]
        key_heads = key_block.reshape(count_keys, local_heads, key_width)
        value_heads = value_block.reshape(count_keys, local_heads, value_width)
        key_pos = first_key + jnp.arange(count_keys, dtype=jnp.int32)
        distance = jnp.abs(query_pos[:, None] - key_pos[None, :]).astype(jnp.float32)
        replaced = (key_pos[None, :] >= query_start[:, None]) & (
            key_pos[None, :] < query_start[:, None] + W
        )
        scores = (
            jnp.einsum("qhd,nhd->qhn", query_flat, key_heads, preferred_element_type=jnp.float32)
            * inverse_root
            - head_slopes[None, :, None] * distance[:, None, :]
        )
        scores = jnp.where(replaced[:, None, :], -jnp.inf, scores)
        new_peak = jnp.maximum(best_score, jnp.max(scores, axis=-1))
        factor = jnp.exp(best_score - new_peak)
        weights = jnp.exp(scores - new_peak[..., None])
        new_total = running_total * factor + jnp.sum(weights, axis=-1)
        new_sum = running_sum * factor[..., None] + jnp.einsum(
            "qhn,nhd->qhd",
            weights.astype(jnp.bfloat16),
            value_heads,
            preferred_element_type=jnp.float32,
        )
        return (new_peak, new_total, new_sum)

    key_part = lax.all_gather(ref_keys, "seq", axis=0, tiled=True)
    value_part = lax.all_gather(ref_values, "seq", axis=0, tiled=True)
    count_keys = key_part.shape[0]
    step_rows = math.gcd(count_keys, 512)
    steps_count = count_keys // step_rows

    def advance(state_now, item_block):
        key_block, value_block, block_first = item_block
        return (absorb(state_now, key_block, value_block, block_first), None)

    firsts = step_rows * jnp.arange(steps_count, dtype=jnp.int32)
    state_out, _ = lax.scan(
        advance,
        initial,
        (
            key_part.reshape(steps_count, step_rows, -1),
            value_part.reshape(steps_count, step_rows, -1),
            firsts,
        ),
    )
    best_score, running_total, running_sum = state_out
    output = (running_sum / running_total[..., None]).astype(jnp.bfloat16)
    return output.reshape(variants, W, local_heads * value_width)


def solution(mesh):
    placed = (
        P(("grp", "seq", "var"), None, None),
        P(("grp", "seq", "var"), None),
        P("grp"),
        P(("grp", "seq", "var"), None),
        P(("grp", "seq", "var")),
        P(("grp", "seq", "var")),
        P(("grp", "seq", "var"), None),
        P(),
        P(),
        P(None, "rep"),
        P(None, "rep"),
        P(None, "rep"),
        P(("grp", "seq"), "rep"),
        P(("grp", "seq"), "rep"),
        P("rep"),
    )
    return jax.shard_map(
        on_device,
        mesh=mesh,
        in_specs=placed,
        out_specs=P(("grp", "seq", "var"), None, "rep"),
        check_vma=False,
    )
```

profile of v0, /device:TPU:0, one launch (start us, length us, event | category | flops | bytes accessed | tf_op | source)
XLA Modules:
  0.0 139.5 jit_solution(10776156495437775536)
XLA Ops:
  6.6 1.3 gather_fusion
  8.4 0.1 broadcast_in_dim.156
  8.5 0.7 gather_fusion.1
  9.2 0.2 convert_reduce_fusion
  9.4 0.2 select_reduce_fusion
  9.6 13.5 %all_to_all.16 = s32[8,1,8]{2,1,0:T(1,128)S(1)} all-to-all(s32[8,1,8]{2,1,0:T(1,128)S(1)} %bitcast.123), channel_id=1, replica_groups=mesh['grp'=2,'seq'=4,'var'=2,'rep'=2] {'seq','var'}, dimensions={0} | all-to-all | bytes 512 | tf_op jit(solution)/shard_map/all_to_all | solution.py:60
  23.3 0.6 gather_fusion.2
  24.0 1.4 %select_select_fusion = bf16[8,8,8,1536]{3,2,1,0:T(8,128)(2,1)} fusion(bf16[8,8,8,1536]{3,2,1,0:T(8,128)(2,1)S(1)} %bitcast.113, pred[8,8]{1,0:T(8,128)(4,1)S(1)} %compare_and_fusion.1, pred[8,8]{1,0:T(8,128)(4,1)S(1)} %compare_bitcast_fusion), kind=kLoop, calls=%fused_computation.64 | loop fusion | flops 1572864 | bytes 3145856 | tf_op jit(solution)/shard_map/jit(_where)/select_n | solution.py:63
  25.4 3.7 %all-to-all-start.1 = ((bf16[8,8,8,1536]{3,2,1,0:T(8,128)(2,1)}), bf16[8,8,8,1536]{3,2,1,0:T(8,128)(2,1)S(1)}, u32[]{:S(2)}, u32[]{:S(2)}) async-start(bf16[8,8,8,1536]{3,2,1,0:T(8,128)(2,1)} %select_select_fusion), calls=%async_computation.1 | async-start | bytes 3145728 | tf_op jit(solution)/shard_map/all_to_all | solution.py:70
  29.3 0.1 broadcast_in_dim.165
  29.7 0.1 compare_and_fusion.2
  29.8 0.7 copy.131
  30.5 0.6 pad_clamp_fusion
  31.1 0.9 slice_reduce_fusion.16
  32.0 43.6 %all_gather.14 = bf16[1024,256]{1,0:T(8,128)(2,1)} all-gather(bf16[256,256]{1,0:T(8,128)(2,1)S(1)} %copy-done.9), channel_id=1, replica_groups=mesh['grp'=2,'seq'=4,'var'=2,'rep'=2] {'seq'}, dimensions={0}, use_global_device_ids=true | all-gather | bytes 655360 | tf_op jit(solution)/shard_map/all_gather | solution.py:174
  75.7 0.7 fusion.41
  76.4 1.4 %gather_fusion.4 = bf16[64,1536]{1,0:T(8,128)(2,1)} fusion(bf16[16,1536]{1,0:T(8,128)(2,1)S(1)} %copy-done.2, s32[1024]{0:T(1024)S(1)} %pad_clamp_fusion.1), kind=kCustom, calls=%fused_computation.4 | custom fusion | bytes 393472 | tf_op jit(solution)/shard_map/jit(_take)/gather | solution.py:67
  77.8 0.7 gather_fusion.3
  78.6 1.8 %broadcast_select_fusion = bf16[16,2,1,8,1536]{4,3,2,1,0:T(8,128)(2,1)} fusion(bf16[16,2,1,8,1536]{4,3,2,1,0:T(8,128)(2,1)S(1)} %bitcast.116, pred[16,2]{1,0:T(8,128)(4,1)} %copy.131), kind=kLoop, calls=%fused_computation.72 | loop fusion | flops 393216 | bytes 1572896 | tf_op jit(solution)/shard_map/jit(_take)/select_n | solution.py:74
  80.4 0.8 fusion.35
  81.2 4.9 %all-to-all-start.2 = ((bf16[8,8,1536]{2,1,0:T(8,128)(2,1)}), bf16[8,8,1536]{2,1,0:T(8,128)(2,1)S(1)}, u32[]{:S(2)}, u32[]{:S(2)}) async-start(bf16[8,8,1536]{2,1,0:T(8,128)(2,1)} %fusion.35), calls=%async_computation.2 | async-start | bytes 393216 | tf_op jit(solution)/shard_map/all_to_all | solution.py:71
  86.2 19.5 %all_gather.15 = bf16[1024,384]{1,0:T(8,128)(2,1)} all-gather(bf16[256,384]{1,0:T(8,128)(2,1)S(1)} %copy-done.8), channel_id=1, replica_groups=mesh['grp'=2,'seq'=4,'var'=2,'rep'=2] {'seq'}, dimensions={0}, use_global_device_ids=true | all-gather | bytes 983040 | tf_op jit(solution)/shard_map/all_gather | solution.py:175
  105.7 0.9 gather_fusion.5
  106.7 1.9 %all_gather.13 = bf16[16,2,2,1536]{3,0,2,1:T(8,128)(2,1)S(1)} all-gather(bf16[16,2,1,1536]{3,0,2,1:T(8,128)(2,1)S(1)} %copy_select_fusion), channel_id=1, replica_groups=mesh['grp'=2,'seq'=4,'var'=2,'rep'=2] {'rep'}, dimensions={2}, use_global_device_ids=true | all-gather | bytes 294912 | tf_op jit(solution)/shard_map/all_gather | solution.py:85
  108.7 0.3 copy.137
  109.2 1.9 %fusion.12 = f32[16,32,1536]{2,1,0:T(8,128)S(1)} fusion(bf16[16,2,2,8,1536]{4,3,2,1,0:T(8,128)(2,1)} %all-gather.2.cloned.1.call-done, f32[16,1536]{1,0:T(8,128)S(1)} %convert_element_type.74, f32[16,32]{1,0:T(8,128)S(1)} %copy-done.13, f32[16,4,1536]{2,1,0:T(4,128)S(1)} %copy.137), kind=kLoop, calls=%fused_computation.28 | loop fusion | flops 3145728 | bytes 5212160 | tf_op jit(solution)/shard_map/add | solution.py:98
  111.3 4.2 %multiply_reduce_fusion = (f32[16,16]{1,0:T(8,128)S(1)}, f32[16,16,1536]{2,1,0:T(8,128)S(1)}) fusion(f32[16,32,1536]{2,1,0:T(8,128)S(1)} %fusion.12, f32[1536]{0:T(1024)S(1)} %copy-done.15, f32[1536]{0:T(1024)S(1)} %copy-done.16, f32[1536]{0:T(1024)S(1)} %copy-done.17, f32[1536]{0:T(1024)S(1)} %copy-done.18, f32[1536]{0:T(1024)S(1)} %copy-done.19, ...), kind=kLoop, calls=%fused_computation.63 | loop fusion | flops 14155520 | bytes 28417024 | tf_op jit(solution)/shard_map/reduce_sum | solution.py:103
  115.6 0.2 multiply_convert_fusion
  115.8 0.9 copy-done.6
  116.7 0.4 convolution_convert_fusion.1
  117.1 0.1 copy.138
  117.3 0.4 convolution_convert_fusion.2
  117.7 0.6 convolution_convert_fusion
  118.3 0.2 reshape.656
  118.5 0.2 fusion.47
  118.7 0.1 fusion.34
  118.8 0.3 convolution_bitcast_fusion.1
  119.2 0.2 copy.146
  119.5 0.8 copy.148
  120.3 11.3 %while.16 = (s32[]{:T(128)}, f32[256,2]{0,1:T(2,128)S(1)}, f32[256,2]{0,1:T(2,128)S(1)}, f32[256,2,192]{0,2,1:T(8,128)S(1)}, s32[2]{0:T(128)S(1)}, /*index=5*/bf...) while((s32[]{:T(128)}, f32[256,2]{0,1:T(2,128)S(1)}, ...), condition=%wide.region_8.9_spmd.clone.clone, body=%wide.region_5.8_spmd.clone.clone.sunk | while | flops 171116544 | bytes 11847073 | solution.py:185
  120.3 0.7 dynamic_slice.25
  121.0 0.7 iota_add_fusion.5
  121.8 0.2 compare_and_fusion.5
  122.2 0.2 abs_convert_fusion.3
  122.3 1.0 constant_dynamic-slice_fusion.4
  123.3 0.1 copy.169
  123.5 1.4 %fusion.68 = (f32[256,2]{0,1:T(2,128)S(1)}, f32[256,2,512]{0,2,1:T(8,128)S(1)}) fusion(f32[256,512]{0,1:T(8,128)S(1)} %abs_convert_fusion.3, f32[2]{0:T(128)S(1)} %get-tuple-element.324, bf16[512,2,128]{0,2,1:T(8,128)(2,1)S(1)} %bitcast.108, bf16[256,2,128]{2,0,1:T(8,128)(2,1)} %get-tuple-element.323, pred[256,512]{0,1:T(8,128)(4,1)S(1)} %compare_and_fusion.5), kind=kOutput, calls=%fused_computation.155.clone.1 | convolution fusion | flops 68419072 | bytes 2099208 | tf_op jit(solution)/shard_map/while/body/eval_jaxpr/qhd,nhd->qhn/dot_general | solution.py:157
  124.9 0.2 fusion.69
  125.1 0.2 copy.170
  125.3 0.4 fusion.70
  125.8 0.1 copy-done.42
  125.9 0.7 dynamic_slice.25
  126.6 0.7 iota_add_fusion.5
  127.5 0.2 compare_and_fusion.5
  127.8 0.2 abs_convert_fusion.3
  128.0 1.0 constant_dynamic-slice_fusion.4
  128.9 0.1 copy.169
  129.1 1.4 %fusion.68 = (f32[256,2]{0,1:T(2,128)S(1)}, f32[256,2,512]{0,2,1:T(8,128)S(1)}) fusion(f32[256,512]{0,1:T(8,128)S(1)} %abs_convert_fusion.3, f32[2]{0:T(128)S(1)} %get-tuple-element.324, bf16[512,2,128]{0,2,1:T(8,128)(2,1)S(1)} %bitcast.108, bf16[256,2,128]{2,0,1:T(8,128)(2,1)} %get-tuple-element.323, pred[256,512]{0,1:T(8,128)(4,1)S(1)} %compare_and_fusion.5), kind=kOutput, calls=%fused_computation.155.clone.1 | convolution fusion | flops 68419072 | bytes 2099208 | tf_op jit(solution)/shard_map/while/body/eval_jaxpr/qhd,nhd->qhn/dot_general | solution.py:157
  130.5 0.2 fusion.69
  130.8 0.2 copy.170
  131.0 0.4 fusion.70
  131.4 0.1 copy-done.42
  131.6 0.2 copy.150
  131.8 0.8 reshape.660
  (155 shorter events, 2.7 us)
Async XLA Ops:
  6.5 111.2 %copy-start = (bf16[1536,384]{1,0:T(8,128)(2,1)S(1)}, bf16[1536,384]{1,0:T(8,128)(2,1)}, u32[]{:S(2)}) copy-start(bf16[1536,384]{1,0:T(8,128)(2,1)} %param.28) | copy-start | bytes 3538948
  6.5 1.9 %copy-start.1 = (s32[128]{0:T(128)S(1)}, s32[128]{0:T(128)}, u32[]{:S(2)}) copy-start(s32[128]{0:T(128)} %param.19) | copy-start | bytes 1540
  8.5 14.8 %copy-start.4 = (bf16[16,8,1536]{2,1,0:T(8,128)(2,1)S(1)}, bf16[16,8,1536]{2,1,0:T(8,128)(2,1)}, u32[]{:S(2)}) copy-start(bf16[16,8,1536]{2,1,0:T(8,128)(2,1)} %param.17) | copy-start | bytes 1179652
  23.2 0.8 copy-start.33
  23.2 0.8 copy-start.35
  25.4 5.1 %copy-start.10 = (bf16[17,1536]{1,0:T(8,128)(2,1)S(1)}, bf16[17,1536]{1,0:T(8,128)(2,1)}, u32[]{:S(2)}) copy-start(bf16[17,1536]{1,0:T(8,128)(2,1)} %param.24) | copy-start | bytes 156676
  25.4 6.6 %copy-start.9 = (bf16[256,256]{1,0:T(8,128)(2,1)S(1)}, bf16[256,256]{1,0:T(8,128)(2,1)}, u32[]{:S(2)}) copy-start(bf16[256,256]{1,0:T(8,128)(2,1)} %param.29) | copy-start | bytes 393220
  25.4 50.3 %copy-start.40 = (s32[16]{0:T(128)S(1)}, s32[16]{0:T(128)}, u32[]{:S(2)}) copy-start(s32[16]{0:T(128)} %param.22) | copy-start | bytes 196
  25.4 50.9 %copy-start.31 = (f32[2]{0:T(128)S(1)}, f32[2]{0:T(128)}, u32[]{:S(2)}) copy-start(f32[2]{0:T(128)} %param.31) | copy-start | bytes 28
  25.4 51.0 %copy-start.2 = (bf16[16,1536]{1,0:T(8,128)(2,1)S(1)}, bf16[16,1536]{1,0:T(8,128)(2,1)}, u32[]{:S(2)}) copy-start(bf16[16,1536]{1,0:T(8,128)(2,1)} %param.18) | copy-start | bytes 147460
  25.4 52.4 %all-to-all-start.1 = ((bf16[8,8,8,1536]{3,2,1,0:T(8,128)(2,1)}), bf16[8,8,8,1536]{3,2,1,0:T(8,128)(2,1)S(1)}, u32[]{:S(2)}, u32[]{:S(2)}) async-start(bf16[8,8,8,1536]{3,2,1,0:T(8,128)(2,1)} %select_select_fusion), calls=%async_computation.1 | async-start | bytes 3145728 | tf_op jit(solution)/shard_map/all_to_all | solution.py:70
  29.2 80.0 %all-gather.2.cloned.1.call-start = ((), (), s32[]{:S(2)}) async-start(), calls=%async_computation.3 | async-start | bytes 2359296 | tf_op jit(solution)/shard_map/all_gather | solution.py:79
  29.8 48.0 %copy-start.38 = (pred[16,2]{0,1:T(4,128)(4,1)}, pred[16,2]{0,1:T(4,128)(4,1)S(1)}, u32[]{:S(2)}) copy-start(pred[16,2]{0,1:T(4,128)(4,1)S(1)} %compare_and_fusion.2) | copy-start | bytes 100
  78.5 1.9 %copy-start.5 = (bf16[64,1536]{1,0:T(8,128)(2,1)S(1)}, bf16[64,1536]{1,0:T(8,128)(2,1)}, u32[]{:S(2)}) copy-start(bf16[64,1536]{1,0:T(8,128)(2,1)} %gather_fusion.4) | copy-start | bytes 589828
  78.6 1.9 %copy-start.34 = (pred[8,8]{1,0:T(8,128)(4,1)S(1)}, pred[8,8]{1,0:T(8,128)(4,1)}, u32[]{:S(2)}) copy-start(pred[8,8]{1,0:T(8,128)(4,1)} %copy-done.33) | copy-start | bytes 196
  78.6 1.9 %copy-start.36 = (pred[8,8]{1,0:T(8,128)(4,1)S(1)}, pred[8,8]{1,0:T(8,128)(4,1)}, u32[]{:S(2)}) copy-start(pred[8,8]{1,0:T(8,128)(4,1)} %copy-done.35) | copy-start | bytes 196
  78.6 7.6 %copy-start.12 = (bf16[16,1536]{1,0:T(8,128)(2,1)S(1)}, bf16[16,1536]{1,0:T(8,128)(2,1)}, u32[]{:S(2)}) copy-start(bf16[16,1536]{1,0:T(8,128)(2,1)} %param.23) | copy-start | bytes 147460
  78.6 7.6 %copy-start.8 = (bf16[256,384]{1,0:T(8,128)(2,1)S(1)}, bf16[256,384]{1,0:T(8,128)(2,1)}, u32[]{:S(2)}) copy-start(bf16[256,384]{1,0:T(8,128)(2,1)} %param.30) | copy-start | bytes 589828
  80.4 26.2 %copy-start.39 = (pred[16,2]{0,1:T(4,128)(4,1)S(1)}, pred[16,2]{0,1:T(4,128)(4,1)}, u32[]{:S(2)}) copy-start(pred[16,2]{0,1:T(4,128)(4,1)} %copy-done.38) | copy-start | bytes 100
  81.2 24.5 %all-to-all-start.2 = ((bf16[8,8,1536]{2,1,0:T(8,128)(2,1)}), bf16[8,8,1536]{2,1,0:T(8,128)(2,1)S(1)}, u32[]{:S(2)}, u32[]{:S(2)}) async-start(bf16[8,8,1536]{2,1,0:T(8,128)(2,1)} %fusion.35), calls=%async_computation.2 | async-start | bytes 393216 | tf_op jit(solution)/shard_map/all_to_all | solution.py:71
  105.7 3.5 %copy-start.13 = (f32[16,32]{1,0:T(8,128)S(1)}, f32[16,32]{1,0:T(8,128)}, u32[]{:S(2)}) copy-start(f32[16,32]{1,0:T(8,128)} %fusion.41) | copy-start | bytes 6148
  109.0 2.1 %copy-start.14 = (f32[1536]{0:T(1024)S(1)}, f32[1536]{0:T(1024)}, u32[]{:S(2)}) copy-start(f32[1536]{0:T(1024)} %get-tuple-element.177) | copy-start | bytes 18436
  109.0 2.1 %copy-start.15 = (f32[1536]{0:T(1024)S(1)}, f32[1536]{0:T(1024)}, u32[]{:S(2)}) copy-start(f32[1536]{0:T(1024)} %get-tuple-element.178) | copy-start | bytes 18436
  109.0 2.1 %copy-start.16 = (f32[1536]{0:T(1024)S(1)}, f32[1536]{0:T(1024)}, u32[]{:S(2)}) copy-start(f32[1536]{0:T(1024)} %get-tuple-element.179) | copy-start | bytes 18436
  109.0 2.1 %copy-start.17 = (f32[1536]{0:T(1024)S(1)}, f32[1536]{0:T(1024)}, u32[]{:S(2)}) copy-start(f32[1536]{0:T(1024)} %get-tuple-element.180) | copy-start | bytes 18436
  109.0 2.1 %copy-start.18 = (f32[1536]{0:T(1024)S(1)}, f32[1536]{0:T(1024)}, u32[]{:S(2)}) copy-start(f32[1536]{0:T(1024)} %get-tuple-element.181) | copy-start | bytes 18436
  109.1 2.1 %copy-start.19 = (f32[1536]{0:T(1024)S(1)}, f32[1536]{0:T(1024)}, u32[]{:S(2)}) copy-start(f32[1536]{0:T(1024)} %get-tuple-element.182) | copy-start | bytes 18436
  109.1 2.1 %copy-start.20 = (f32[1536]{0:T(1024)S(1)}, f32[1536]{0:T(1024)}, u32[]{:S(2)}) copy-start(f32[1536]{0:T(1024)} %get-tuple-element.183) | copy-start | bytes 18436
  109.1 2.1 %copy-start.21 = (f32[1536]{0:T(1024)S(1)}, f32[1536]{0:T(1024)}, u32[]{:S(2)}) copy-start(f32[1536]{0:T(1024)} %get-tuple-element.184) | copy-start | bytes 18436
  109.1 2.1 %copy-start.22 = (f32[1536]{0:T(1024)S(1)}, f32[1536]{0:T(1024)}, u32[]{:S(2)}) copy-start(f32[1536]{0:T(1024)} %get-tuple-element.185) | copy-start | bytes 18436
  109.1 2.1 %copy-start.23 = (f32[1536]{0:T(1024)S(1)}, f32[1536]{0:T(1024)}, u32[]{:S(2)}) copy-start(f32[1536]{0:T(1024)} %get-tuple-element.186) | copy-start | bytes 18436
  109.1 2.1 %copy-start.24 = (f32[1536]{0:T(1024)S(1)}, f32[1536]{0:T(1024)}, u32[]{:S(2)}) copy-start(f32[1536]{0:T(1024)} %get-tuple-element.187) | copy-start | bytes 18436
  109.1 2.1 %copy-start.25 = (f32[1536]{0:T(1024)S(1)}, f32[1536]{0:T(1024)}, u32[]{:S(2)}) copy-start(f32[1536]{0:T(1024)} %get-tuple-element.188) | copy-start | bytes 18436
  109.1 2.1 %copy-start.26 = (f32[1536]{0:T(1024)S(1)}, f32[1536]{0:T(1024)}, u32[]{:S(2)}) copy-start(f32[1536]{0:T(1024)} %get-tuple-element.189) | copy-start | bytes 18436
  109.1 2.1 %copy-start.27 = (f32[1536]{0:T(1024)S(1)}, f32[1536]{0:T(1024)}, u32[]{:S(2)}) copy-start(f32[1536]{0:T(1024)} %get-tuple-element.190) | copy-start | bytes 18436
  109.1 2.1 %copy-start.28 = (f32[1536]{0:T(1024)S(1)}, f32[1536]{0:T(1024)}, u32[]{:S(2)}) copy-start(f32[1536]{0:T(1024)} %get-tuple-element.191) | copy-start | bytes 18436
  109.2 2.1 %copy-start.29 = (f32[1536]{0:T(1024)S(1)}, f32[1536]{0:T(1024)}, u32[]{:S(2)}) copy-start(f32[1536]{0:T(1024)} %get-tuple-element.192) | copy-start | bytes 18436
  109.2 2.1 %copy-start.30 = (f32[1536]{0:T(1024)S(1)}, f32[1536]{0:T(1024)}, u32[]{:S(2)}) copy-start(f32[1536]{0:T(1024)} %get-tuple-element.193) | copy-start | bytes 18436
  111.3 4.3 %copy-start.37 = (f32[1536]{0:T(1024)S(1)}, f32[1536]{0:T(1024)}, u32[]{:S(2)}) copy-start(f32[1536]{0:T(1024)} %param.25) | copy-start | bytes 18436
  115.6 1.1 copy-start.6
  115.8 1.5 %copy-start.7 = (bf16[1536,256]{1,0:T(8,128)(2,1)S(1)}, bf16[1536,256]{1,0:T(8,128)(2,1)}, u32[]{:S(2)}) copy-start(bf16[1536,256]{1,0:T(8,128)(2,1)} %param.27) | copy-start | bytes 2359300
  118.8 1.5 %copy-start.11 = (s32[16]{0:T(128)S(1)}, s32[16]{0:T(128)}, u32[]{:S(2)}) copy-start(s32[16]{0:T(128)} %param.21) | copy-start | bytes 196
  118.8 1.5 %copy-start.32 = (f32[2]{0:T(128)S(1)}, f32[2]{0:T(128)}, u32[]{:S(2)}) copy-start(f32[2]{0:T(128)} %param.31) | copy-start | bytes 28
  120.3 1.8 %copy-start.41 = (s32[2]{0:T(128)}, s32[2]{0:T(128)S(1)}, u32[]{:S(2)}) copy-start(s32[2]{0:T(128)S(1)} %get-tuple-element.321) | copy-start | bytes 28 | tf_op jit(solution)/shard_map/while
  123.5 1.6 %copy-start.3 = (bf16[2,512,384]{2,1,0:T(8,128)(2,1)S(1)}, bf16[2,512,384]{2,1,0:T(8,128)(2,1)}, u32[]{:S(2)}) copy-start(bf16[2,512,384]{2,1,0:T(8,128)(2,1)} %get-tuple-element.325) | copy-start | bytes 2359300 | tf_op jit(solution)/shard_map/while
  125.3 0.6 copy-start.42
  125.9 1.8 %copy-start.41 = (s32[2]{0:T(128)}, s32[2]{0:T(128)S(1)}, u32[]{:S(2)}) copy-start(s32[2]{0:T(128)S(1)} %get-tuple-element.321) | copy-start | bytes 28 | tf_op jit(solution)/shard_map/while
  129.1 1.6 %copy-start.3 = (bf16[2,512,384]{2,1,0:T(8,128)(2,1)S(1)}, bf16[2,512,384]{2,1,0:T(8,128)(2,1)}, u32[]{:S(2)}) copy-start(bf16[2,512,384]{2,1,0:T(8,128)(2,1)} %get-tuple-element.325) | copy-start | bytes 2359300 | tf_op jit(solution)/shard_map/while
  131.0 0.6 copy-start.42
Sparse Core Ops, SparseCore 0:
  80.5 10.1 all-gather.1
where the time goes:
time: 140 us; the launch traced here: 139 us
  blocking collectives  78.6 us (56%)
  local copies, waits for them, and re-layouts  16.9 us (12%)
  other arithmetic  15.2 us (11%)
  between operations  14.2 us (10%)
  starting transfers between devices  8.68 us (6%)
  matrix products  5.54 us (4%)
    all_gather x1, blocking collectives, on_device(): key_part = lax.all_gather(ref_keys, 'seq', axis=0, tiled=True)  43.6 us
    all_gather x1, blocking collectives, on_device(): value_part = lax.all_gather(ref_values, 'seq', axis=0, tiled=True)  19.5 us
    all_to_all x1, blocking collectives, on_device(): lax.all_to_all(request_rows, ('seq', 'var'), split_axis=0, concat_axis=0,...  13.5 us
    all_to_all x1, starting transfers between devices, on_device(): lax.all_to_all(send_scales, ('seq', 'var'), split_axis=0, concat_axis=0,...  4.92 us
    reduce_sum x1, other arithmetic, on_device(): mean_square = jnp.mean(tower_rows * tower_rows, axis=-1, keepdims=True)  4.24 us
    dynamic_slice x10, local copies, waits for them, and re-layouts, on_device(): lax.scan(advance, initial, (key_part.reshape(steps_count, step_rows, -1),...  4.03 us
    all_to_all x1, starting transfers between devices, on_device(): lax.all_to_all(send_blocks, ('seq', 'var'), split_axis=0, concat_axis=0,...  3.72 us
    dot_general x2, matrix products, absorb(): jnp.einsum('qhd,nhd->qhn', query_flat, key_heads, preferred_element_type=...  2.8 us
  transfers between devices with their start and end apart: 3, of which 0 were waited for; matrix products, arithmetic and copies ran while one was open for 5% of the time, Pallas kernels for 0%

commit v1 on v0

v1 whole, which is shorter than its diff:
```python
import functools
import math

import jax
import jax.numpy as jnp
from jax import lax
from jax.experimental import pallas as pl
from jax.experimental.pallas import tpu as pltpu
from jax.sharding import PartitionSpec as P

W = 16
RADIUS = 8
TAPS = 2 * RADIUS + 1
EPSILON = 1e-06
PARTS = 4


def send(x, seq_mask, var_mask=0):
    seq, var = lax.axis_size("seq"), lax.axis_size("var")
    pairs = [
        (p * var + q, (p ^ seq_mask) * var + (q ^ var_mask))
        for p in range(seq)
        for q in range(var)
    ]
    return lax.ppermute(x, ("seq", "var"), pairs)


def then(*arrays):
    return lax.optimization_barrier(arrays)


def pack_kernel(vals, scales, cells):
    per_owner, half = scales.shape
    cells[pl.ds(0, per_owner)] = vals[...]
    rows = scales[...].astype(jnp.float32)
    missing = (cells.shape[0] - per_owner) * 8 - per_owner
    if missing:
        rows = jnp.concatenate([rows, jnp.zeros((missing, half), jnp.float32)], axis=0)
    rows = rows.reshape(-1, 8, half).astype(jnp.bfloat16)
    cells[pl.ds(per_owner, rows.shape[0])] = rows


def gather_all(cells, window, *small):
    seq, var = lax.axis_size("seq"), lax.axis_size("var")
    me_var = lax.axis_index("var")
    if not on_line(seq, var):
        cells = lax.all_gather(cells, ("seq", "var"), axis=0, tiled=False)
        return [cells], [lax.all_gather(window, "seq", axis=0, tiled=True)], small
    part = window.shape[0] // 2

    cells_1, across, cells_3 = send(cells, 1), send(cells, 0, 1), send(cells, 3)
    cells_1, across, window = then(cells_1, across, window)
    share = lax.dynamic_slice_in_dim(window, me_var * part, part, axis=0)
    across_1 = send(cells_1, 0, 1)
    cells_3, *small = then(cells_3, *small)
    cells_2 = send(cells_3, 1)
    cells_3, across_1 = then(cells_3, across_1)
    across_3 = send(cells_3, 0, 1)
    cells_2, share = then(cells_2, share)
    across_2, share_2 = send(cells_2, 0, 1), send(share, 2)
    across_3, share = then(across_3, share)
    share_1 = send(share, 1)
    share_3 = send(share_2, 1)
    share_across_2, share_across_1 = send(share_2, 0, 1), send(share_1, 0, 1)
    share_across_3 = send(share_3, 0, 1)

    pieces = [cells, across, cells_1, across_1, cells_2, across_2, cells_3, across_3]
    windows = [
        window,
        share_1,
        share_across_1,
        share_2,
        share_across_2,
        share_3,
        share_across_3,
    ]
    return [piece[None] for piece in pieces], windows, small


def on_line(seq, var):
    return seq == 4 and var == 2


def place_of(owner):
    seq, var = lax.axis_size("seq"), lax.axis_size("var")
    if not on_line(seq, var):
        return owner
    return owner ^ (lax.axis_index("seq") * var + lax.axis_index("var"))


def first_keys(rows):
    seq, var = lax.axis_size("seq"), lax.axis_size("var")
    me_seq, me_var = lax.axis_index("seq"), lax.axis_index("var")
    if not on_line(seq, var):
        return [[rows * p for p in range(seq)]]
    firsts = [[me_seq * rows]]
    for mask in (1, 2, 3):
        for side in (0, 1):
            firsts.append([(me_seq ^ mask) * rows + (me_var ^ side) * (rows // 2)])
    return firsts


def tower_kernel(
    per_owner,
    block_slot,
    block_lists,
    window_offsets,
    deltas,
    taps,
    *rest,
):
    *rest, held, taps32, deltas32 = rest
    pieces, outs = rest[:-PARTS], rest[-PARTS:]
    channels = taps32.shape[2]
    taps32[...] = jnp.broadcast_to(taps[...].astype(jnp.float32)[:, None, :], taps32.shape)
    deltas32[...] = deltas[...].astype(jnp.float32)
    first = 0
    for piece in pieces:
        scale_cells = piece.shape[1] - per_owner
        for p in range(piece.shape[0]):
            scale = piece[p, pl.ds(per_owner, scale_cells)].astype(jnp.float32)
            scale = scale.reshape(scale_cells * 8, channels)
            for i in range(per_owner):
                held[first + i] = piece[p, i].astype(jnp.float32) * scale[i : i + 1]
            first += per_owner
    chunk = 256
    row = lax.broadcasted_iota(jnp.int32, (8, chunk), 0)

    def variant(out, begin, v):
        places = []
        for k in range(4):
            slot = block_slot[block_lists[k, begin + v]]
            owner = slot // per_owner
            places.append(place_of(owner) * per_owner + slot - owner * per_owner)
        offset = window_offsets[begin + v]
        for at in range(0, channels, chunk):
            lanes = slice(at, at + chunk)
            cells = [held[place, :, lanes] for place in places]
            delta = deltas32[pl.ds(begin + v, 1), lanes]
            cells[1] = cells[1] + jnp.where(row == offset, delta, 0.0)
            cells[2] = cells[2] + jnp.where(row == offset - 8, delta, 0.0)
            early, late = jnp.stack(cells[:3]), jnp.stack(cells[1:])
            total = None
            for s in range(7, 0, -1):
                term = early * taps32[s, :, lanes] + late * taps32[s + 8, :, lanes]
                total = term if total is None else total + term
                total = pltpu.roll(total.reshape(24, chunk), 23, 0).reshape(3, 8, chunk)
            total = total[0:2] + early[0:2] * taps32[0, :, lanes]
            total = total + late[0:2] * (1.0 + taps32[8, :, lanes])
            total = total + late[1:3] * taps32[16, :, lanes]
            out[pl.ds(pl.multiple_of(v * W, W), W), lanes] = total.reshape(W, chunk)

    begin = 0
    for out in outs:
        pl.loop(0, out.shape[0] // W)(functools.partial(variant, out, begin))
        begin += out.shape[0] // W


def value_window(h, value_width):
    return h * value_width // 128 * 128, -(-(h + 1) * value_width // 128) * 128


def row_starts(positions):
    return jnp.concatenate(
        [jnp.full((W, 1), positions[v], jnp.int32) for v in range(positions.shape[0])], axis=0
    ).astype(jnp.float32)


def scores_of(query, keys):
    product = lax.dot_general(
        query, keys, (((1,), (1,)), ((), ())), preferred_element_type=jnp.float32
    )
    return product * (1.0 / math.sqrt(query.shape[1]))


def key_places(piece, firsts):
    each = piece.shape[0] // len(firsts)
    places = [first + lax.broadcasted_iota(jnp.int32, (1, each), 1) for first in firsts]
    return jnp.concatenate(places, axis=1).astype(jnp.float32)


def piece_scores(h, query, start, place, slope, pieces, firsts):
    width, found = query.shape[1], []
    for piece, first in zip(pieces, firsts):
        key_at = key_places(piece, first)
        score = scores_of(query, piece[:, h * width : (h + 1) * width])
        score = score - slope * jnp.abs(place - key_at)
        kept = jnp.abs(start + (W - 1) / 2 - key_at) > W / 2
        found.append(jnp.where(kept, score, -jnp.inf))
    return found


def weigh(scores, values, peak):
    total, summed = 0.0, 0.0
    for score, value in zip(scores, values):
        weight = jnp.exp(score - peak)
        total = total + jnp.sum(weight, axis=1, keepdims=True)
        summed = summed + jnp.dot(
            weight.astype(jnp.bfloat16), value, preferred_element_type=jnp.float32
        )
    return total, summed


def peak_of(scores):
    return functools.reduce(jnp.maximum, [jnp.max(s, axis=1, keepdims=True) for s in scores])


def near_kernel(
    sizes,
    positions,
    slopes,
    gain,
    w_query,
    w_key,
    w_value,
    *rest,
):
    value_width, window_rows = sizes
    mine, others = rest[:PARTS], rest[PARTS : 2 * PARTS]
    pieces = rest[2 * PARTS : -3]
    queries_out, stats, sums = rest[-3:]
    heads = slopes.shape[0]
    rep = lax.axis_index("rep")
    own = jnp.concatenate([part[...] for part in mine], axis=0)
    far = jnp.concatenate([part[...] for part in others], axis=0)
    rows, half = own.shape
    mean = (
        jnp.sum(own * own, axis=1, keepdims=True) + jnp.sum(far * far, axis=1, keepdims=True)
    ) / (2 * half)
    factor = lax.rsqrt(mean + EPSILON)
    gain_low, gain_high = gain[:, :half], gain[:, half:]
    own = own * factor * jnp.where(rep == 0, gain_low, gain_high)
    far = far * factor * jnp.where(rep == 0, gain_high, gain_low)
    own, far = own.astype(jnp.bfloat16), far.astype(jnp.bfloat16)
    at_own = pl.ds(pl.multiple_of(rep * half, half), half)
    at_far = pl.ds(pl.multiple_of((1 - rep) * half, half), half)

    def project(w):
        return (
            jnp.dot(own, w[at_own, :], preferred_element_type=jnp.float32)
            + jnp.dot(far, w[at_far, :], preferred_element_type=jnp.float32)
        ).astype(jnp.bfloat16)

    queries, own_keys, own_values = project(w_query), project(w_key), project(w_value)
    queries_out[...] = queries
    start = row_starts(positions)
    place = start + (lax.broadcasted_iota(jnp.int32, (rows, 1), 0) % W).astype(jnp.float32)
    at = lax.broadcasted_iota(jnp.int32, (rows, rows), 0)
    to = lax.broadcasted_iota(jnp.int32, (rows, rows), 1)
    together, apart = at // W == to // W, jnp.abs(at - to).astype(jnp.float32)
    width = queries.shape[1] // heads
    for h in range(heads):
        cols = slice(h * width, (h + 1) * width)
        low, high = value_window(h, value_width)
        base = heads * width
        near = scores_of(queries[:, cols], own_keys[:, cols]) - slopes[h] * apart
        scores = [jnp.where(together, near, -jnp.inf)]
        scores += piece_scores(
            h, queries[:, cols], start, place, slopes[h], pieces, first_keys(window_rows)
        )
        values = [own_values[:, low:high]]
        values += [piece[:, base + low : base + high] for piece in pieces]
        peak = peak_of(scores)
        total, summed = weigh(scores, values, peak)
        stats[2 * h] = jnp.broadcast_to(peak, (rows, 128))
        stats[2 * h + 1] = jnp.broadcast_to(total, (rows, 128))
        sums[h] = summed


def far_kernel(sizes, positions, slopes, queries, stats, sums, *rest):
    value_width, window_rows = sizes
    *pieces, out = rest
    firsts = first_keys(window_rows)[-len(pieces) :]
    heads = slopes.shape[0]
    rows, width = queries.shape[0], queries.shape[1] // heads
    start = row_starts(positions)
    place = start + (lax.broadcasted_iota(jnp.int32, (rows, 1), 0) % W).astype(jnp.float32)
    results = []
    for h in range(heads):
        low, high = value_window(h, value_width)
        base = heads * width
        scores = piece_scores(
            h,
            queries[:, h * width : (h + 1) * width],
            start,
            place,
            slopes[h],
            pieces,
            firsts,
        )
        values = [piece[:, base + low : base + high] for piece in pieces]
        before = stats[2 * h][:, :1]
        peak = jnp.maximum(before, peak_of(scores))
        total, summed = weigh(scores, values, peak)
        factor = jnp.exp(before - peak)
        total = total + stats[2 * h + 1][:, :1] * factor
        summed = summed + sums[h] * factor
        results.append((low, high, summed * (1.0 / total)))
    lane = lax.broadcasted_iota(jnp.int32, (rows, 128), 1)
    for column in range(0, heads * value_width, 128):
        merged = None
        for h, (low, high, value) in enumerate(results):
            if low <= column < high:
                part = value[:, column - low : column - low + 128]
                if merged is None:
                    merged = part
                else:
                    merged = jnp.where(lane + column >= h * value_width, part, merged)
        out[:, column : column + 128] = merged.astype(jnp.bfloat16)


def on_device(
    cache_vals,
    cache_scales,
    block_slot,
    block_lists,
    variant_pos,
    window_offsets,
    variant_deltas,
    conv_taps,
    norm_gain,
    w_query,
    w_key,
    w_value,
    ref_keys,
    ref_values,
    head_slopes,
):
    per_owner, block_rows, channels = cache_vals.shape
    variants = block_lists.shape[0]
    half = channels // lax.axis_size("rep")
    smem = pl.BlockSpec(memory_space=pltpu.SMEM)
    vmem = pl.BlockSpec(memory_space=pltpu.VMEM)

    def my_half(x):
        return lax.dynamic_slice_in_dim(x, lax.axis_index("rep") * half, half, axis=x.ndim - 1)

    scales, vals = then(my_half(cache_scales), cache_vals)
    all_cells = per_owner + -(-per_owner // 8)
    cells = pl.pallas_call(
        pack_kernel,
        out_shape=jax.ShapeDtypeStruct((all_cells, block_rows, half), jnp.bfloat16),
        in_specs=[vmem, vmem],
        out_specs=vmem,
        compiler_params=pltpu.CompilerParams(vmem_limit_bytes=4 * 1024 * 1024),
        name="pack",
    )(my_half(vals), scales)
    window = jnp.concatenate([ref_keys, ref_values], axis=1)
    slot_pieces, window_pieces, (deltas, taps, gain) = gather_all(
        cells,
        window,
        my_half(variant_deltas),
        my_half(conv_taps),
        norm_gain.reshape(1, channels),
    )
    held = sum(piece.shape[0] for piece in slot_pieces) * per_owner
    tower_limit = 8 * held * block_rows * half * 4 // 3 + 4 * 1024 * 1024
    tower_shapes = [
        jax.ShapeDtypeStruct(((variants + i) // PARTS * W, half), jnp.float32)
        for i in reversed(range(PARTS))
    ]
    towers = pl.pallas_call(
        functools.partial(tower_kernel, per_owner),
        out_shape=tower_shapes,
        in_specs=[smem, smem, smem] + [vmem] * (2 + len(slot_pieces)),
        out_specs=[vmem] * PARTS,
        scratch_shapes=[
            pltpu.VMEM((held, block_rows, half), jnp.float32),
            pltpu.VMEM((TAPS, 8, half), jnp.float32),
            pltpu.VMEM((variants, half), jnp.float32),
        ],
        compiler_params=pltpu.CompilerParams(vmem_limit_bytes=tower_limit),
        cost_estimate=pl.CostEstimate(
            flops=10**9, bytes_accessed=4 * 10**7, transcendentals=0
        ),
        name="tower",
    )(
        block_slot,
        block_lists.T,
        window_offsets,
        deltas,
        taps,
        *slot_pieces,
    )
    swap = [(0, 1), (1, 0)]
    if len(window_pieces) > 2:
        *towers, window_pieces[5] = then(*towers, window_pieces[5])
        *towers, last = towers
        last, window_pieces[2], window_pieces[4] = then(last, window_pieces[2], window_pieces[4])
        towers = [*towers, last]
    others = [lax.ppermute(tower, "rep", swap) for tower in towers]
    heads, rows = head_slopes.shape[0], variants * W
    value_width = w_value.shape[1] // heads
    cut = len(window_pieces) - 1
    sizes = (value_width, ref_keys.shape[0])
    low, high = value_window(heads - 1, value_width)
    queries, stats, sums = pl.pallas_call(
        functools.partial(near_kernel, sizes),
        out_shape=[
            jax.ShapeDtypeStruct((rows, w_query.shape[1]), jnp.bfloat16),
            jax.ShapeDtypeStruct((2 * heads, rows, 128), jnp.float32),
            jax.ShapeDtypeStruct((heads, rows, high - low), jnp.float32),
        ],
        in_specs=[smem, smem] + [vmem] * (4 + 2 * PARTS + cut),
        out_specs=[vmem] * 3,
        compiler_params=pltpu.CompilerParams(vmem_limit_bytes=20 * 1024 * 1024),
        name="near",
    )(
        variant_pos,
        head_slopes,
        gain,
        w_query,
        w_key,
        w_value,
        *towers,
        *others,
        *window_pieces[:cut],
    )
    output = pl.pallas_call(
        functools.partial(far_kernel, sizes),
        out_shape=jax.ShapeDtypeStruct((rows, w_value.shape[1]), jnp.bfloat16),
        in_specs=[smem, smem] + [vmem] * (3 + len(window_pieces) - cut),
        out_specs=vmem,
        compiler_params=pltpu.CompilerParams(vmem_limit_bytes=20 * 1024 * 1024),
        name="far",
    )(variant_pos, head_slopes, queries, stats, sums, *window_pieces[cut:])
    return output.reshape(variants, W, -1)


def solution(mesh):
    placed = (
        P(("grp", "seq", "var"), None, None),
        P(("grp", "seq", "var"), None),
        P("grp"),
        P(("grp", "seq", "var"), None),
        P(("grp", "seq", "var")),
        P(("grp", "seq", "var")),
        P(("grp", "seq", "var"), None),
        P(),
        P(),
        P(None, "rep"),
        P(None, "rep"),
        P(None, "rep"),
        P(("grp", "seq"), "rep"),
        P(("grp", "seq"), "rep"),
        P("rep"),
    )
    return jax.shard_map(
        on_device,
        mesh=mesh,
        in_specs=placed,
        out_specs=P(("grp", "seq", "var"), None, "rep"),
        check_vma=False,
    )
```

time: 140 us -> 49.4 us (0.35)
  blocking collectives: 78.6 us -> 0 us
  waiting for transfers between devices: 0.04 us -> 17.9 us
  local copies, waits for them, and re-layouts: 16.9 us -> 1.77 us
  other arithmetic: 15.2 us -> 1.03 us
  between operations: 14.2 us -> 0.16 us
  starting transfers between devices: 8.68 us -> 19.7 us
  Pallas kernels: 0 us -> 7.98 us
  matrix products: 5.54 us -> 0 us
    all_gather x3 -> x0, blocking collectives: 65.1 us -> none  [the longest x1 43.6 us: on_device(): key_part = lax.all_gather(ref_keys, 'seq', axis=0, tiled=True)]
    ppermute x0 -> x17, starting transfers between devices: none -> 19.7 us  [the longest x13 18.6 us: send(): return lax.ppermute(x, ('seq', 'var'), pairs)]
    ppermute x0 -> x17, waiting for transfers between devices: none -> 17.9 us  [the longest x13 17.6 us: send(): return lax.ppermute(x, ('seq', 'var'), pairs)]
    all_to_all x1 -> x0, blocking collectives: 13.5 us -> none  [on_device(): lax.all_to_all(request_rows, ('seq', 'var'), split_axis=0, concat_axis=0,...]
    all_to_all x2 -> x0, starting transfers between devices: 8.64 us -> none  [the longest x1 4.92 us: on_device(): lax.all_to_all(send_scales, ('seq', 'var'), split_axis=0, concat_axis=0,...]
    pallas_call x0 -> x4, Pallas kernels: none -> 7.98 us  [the longest x1 3.26 us: on_device(): pl.pallas_call(functools.partial(tower_kernel, per_owner), out_shape=towe...]
    gather x12 -> x0, local copies, waits for them, and re-layouts: 6.15 us -> none  [the longest x4 1.59 us: on_device(): jnp.take(block_lists, columns, axis=1)]
    dot_general x9 -> x0, matrix products: 5.54 us -> none  [the longest x2 2.8 us: absorb(): jnp.einsum('qhd,nhd->qhn', query_flat, key_heads, preferred_element_type=...]
  transfers between devices with their start and end apart: 3 -> 17, of which waited for: 0 -> 10; matrix products, arithmetic and copies ran while one was open for 5% -> 4% of each run, Pallas kernels for 0% -> 13%
where the time goes in v1:
time: 49.4 us; the launch traced here: 48.5 us
  starting transfers between devices  19.7 us (40%)
  waiting for transfers between devices  17.9 us (36%)
  Pallas kernels  7.98 us (16%)
  local copies, waits for them, and re-layouts  1.77 us (4%)
  other arithmetic  1.03 us (2%)
    ppermute x13, starting transfers between devices, send(): return lax.ppermute(x, ('seq', 'var'), pairs)  18.6 us
    ppermute x13, waiting for transfers between devices, send(): return lax.ppermute(x, ('seq', 'var'), pairs)  17.6 us
    pallas_call x1, Pallas kernels, on_device(): pl.pallas_call(functools.partial(tower_kernel, per_owner), out_shape=towe...  3.26 us
    pallas_call x1, Pallas kernels, on_device(): pl.pallas_call(functools.partial(near_kernel, sizes), out_shape=[jax.Shap...  2.87 us
    pallas_call x1, Pallas kernels, on_device(): pl.pallas_call(functools.partial(far_kernel, sizes), out_shape=jax.ShapeD...  1.83 us
    ppermute x4, starting transfers between devices, on_device(): others = [lax.ppermute(tower, 'rep', swap) for tower in towers]  1.08 us
    concatenate x1, other arithmetic, on_device(): window = jnp.concatenate([ref_keys, ref_values], axis=1)  1.03 us
  transfers between devices with their start and end apart: 17, of which 10 were waited for; matrix products, arithmetic and copies ran while one was open for 4% of the time, Pallas kernels for 13%

profile of v1, /device:TPU:0, one launch (start us, length us, event | category | flops | bytes accessed | tf_op | source)
XLA Modules:
  0.0 48.5 jit_solution(3362446778370279688)
XLA Ops:
  0.0 0.0 copy-start
  0.0 0.0 copy-start.10
  0.0 0.0 copy-start.9
  0.0 0.0 copy-start.6
  0.0 0.0 copy-start.7
  0.0 0.0 copy-start.8
  0.0 0.8 %constant_dynamic-slice_fusion.4.scales = bf16[16,768]{1,0:T(8,128)(2,1)S(1)} fusion(bf16[16,1536]{1,0:T(8,128)(2,1)} %param.16, s32[]{:T(128)S(6)} %select_n.4), kind=kLoop, calls=%fused_computation.5 | loop fusion | bytes 49156 | tf_op jit(solution)/shard_map/dynamic_slice | solution.py:336
  0.8 0.2 copy-done
  1.1 3.1 %collective-permute-start.1 = (bf16[18,8,768]{2,1,0:T(8,128)(2,1)S(1)}, bf16[18,8,768]{2,1,0:T(8,128)(2,1)S(1)}, u32[]{:S(2)}, u32[]{:S(2)}) collective-permute-start(bf16[18,8,768]{2,1,0:T(8,128)(2,1)S(1)} %pack.1), channel_id=1, source_target_pairs={{0,4},{2,6},{4,0},{6,2},{8,12},{10,14},{12,8},{14,10},{1,5},{3,7},... | collective-permute-start | bytes 663560 | tf_op jit(solution)/shard_map/ppermute | solution.py:25
  4.1 1.5 %collective-permute-start.2 = (bf16[18,8,768]{2,1,0:T(8,128)(2,1)S(1)}, bf16[18,8,768]{2,1,0:T(8,128)(2,1)S(1)}, u32[]{:S(2)}, u32[]{:S(2)}) collective-permute-start(bf16[18,8,768]{2,1,0:T(8,128)(2,1)S(1)} %pack.1), channel_id=1, source_target_pairs={{0,2},{2,0},{4,6},{6,4},{8,10},{10,8},{12,14},{14,12},{1,3},{3,1},... | collective-permute-start | bytes 663560 | tf_op jit(solution)/shard_map/ppermute | solution.py:25
  5.6 2.5 %collective-permute-start = (bf16[18,8,768]{2,1,0:T(8,128)(2,1)S(1)}, bf16[18,8,768]{2,1,0:T(8,128)(2,1)S(1)}, u32[]{:S(2)}, u32[]{:S(2)}) collective-permute-start(bf16[18,8,768]{2,1,0:T(8,128)(2,1)S(1)} %pack.1), channel_id=1, source_target_pairs={{0,12},{2,14},{4,8},{6,10},{8,4},{10,6},{12,0},{14,2},{1,13},{3,15... | collective-permute-start | bytes 663560 | tf_op jit(solution)/shard_map/ppermute | solution.py:25
  8.1 0.7 %reshape.6.gain = f32[1,1536]{1,0:T(1,128)S(1)} reshape(f32[1536]{0:T(1024)} %param.23) | data formatting | bytes 12288 | tf_op jit(solution)/shard_map/reshape | solution.py:354
  8.8 1.0 %pad_maximum_fusion.rest_8_ = bf16[256,640]{1,0:T(8,128)(2,1)S(1)} fusion(bf16[256,384]{1,0:T(8,128)(2,1)} %param.28, bf16[256,256]{1,0:T(8,128)(2,1)} %param.27), kind=kLoop, calls=%fused_computation | loop fusion | flops 655360 | bytes 655360 | tf_op jit(solution)/shard_map/concatenate | solution.py:348
  9.8 0.1 collective-permute-done.1
  10.0 1.1 %collective-permute-done.2 = bf16[18,8,768]{2,1,0:T(8,128)(2,1)S(1)} collective-permute-done((bf16[18,8,768]{2,1,0:T(8,128)(2,1)S(1)}, bf16[18,8,768]{2,1,0:T(8,128)(2,1)S(1)}, u32[]{:S(2)}, u32[]{:S(2)}) %collective-permute-start.2) | collective-permute-done | bytes 221216 | tf_op jit(solution)/shard_map/ppermute | solution.py:25
  11.0 1.5 %collective-permute-start.3 = (bf16[18,8,768]{2,1,0:T(8,128)(2,1)S(1)}, bf16[18,8,768]{2,1,0:T(8,128)(2,1)S(1)}, u32[]{:S(2)}, u32[]{:S(2)}) collective-permute-start(bf16[18,8,768]{2,1,0:T(8,128)(2,1)S(1)} %collective-permute-done.1), channel_id=1, source_target_pairs={{0,2},{2,0},{4,6},{6,4},{8,10},{10,8},{12,14},{14,12},{1,3},{3,1},... | collective-permute-start | bytes 663560 | tf_op jit(solution)/shard_map/ppermute | solution.py:25
  12.5 0.0 copy-done.10
  12.5 0.0 copy-done.9
  12.6 4.1 %collective-permute-done = bf16[18,8,768]{2,1,0:T(8,128)(2,1)S(1)} collective-permute-done((bf16[18,8,768]{2,1,0:T(8,128)(2,1)S(1)}, bf16[18,8,768]{2,1,0:T(8,128)(2,1)S(1)}, u32[]{:S(2)}, u32[]{:S(2)}) %collective-permute-start) | collective-permute-done | bytes 221216 | tf_op jit(solution)/shard_map/ppermute | solution.py:25
  16.6 1.8 %collective-permute-start.4 = (bf16[18,8,768]{2,1,0:T(8,128)(2,1)S(1)}, bf16[18,8,768]{2,1,0:T(8,128)(2,1)S(1)}, u32[]{:S(2)}, u32[]{:S(2)}) collective-permute-start(bf16[18,8,768]{2,1,0:T(8,128)(2,1)S(1)} %collective-permute-done), channel_id=1, source_target_pairs={{0,4},{2,6},{4,0},{6,2},{8,12},{10,14},{12,8},{14,10},{1,5},{3,7},... | collective-permute-start | bytes 663560 | tf_op jit(solution)/shard_map/ppermute | solution.py:25
  18.4 0.0 collective-permute-done.3
  18.4 0.5 %collective-permute-start.6 = (bf16[18,8,768]{2,1,0:T(8,128)(2,1)S(1)}, bf16[18,8,768]{2,1,0:T(8,128)(2,1)S(1)}, u32[]{:S(2)}, u32[]{:S(2)}) collective-permute-start(bf16[18,8,768]{2,1,0:T(8,128)(2,1)S(1)} %collective-permute-done), channel_id=1, source_target_pairs={{0,2},{2,0},{4,6},{6,4},{8,10},{10,8},{12,14},{14,12},{1,3},{3,1},... | collective-permute-start | bytes 663560 | tf_op jit(solution)/shard_map/ppermute | solution.py:25
  19.0 3.9 %collective-permute-done.4 = bf16[18,8,768]{2,1,0:T(8,128)(2,1)S(1)} collective-permute-done((bf16[18,8,768]{2,1,0:T(8,128)(2,1)S(1)}, bf16[18,8,768]{2,1,0:T(8,128)(2,1)S(1)}, u32[]{:S(2)}, u32[]{:S(2)}) %collective-permute-start.4) | collective-permute-done | bytes 221216 | tf_op jit(solution)/shard_map/ppermute | solution.py:25
  22.8 3.7 %collective-permute-start.7 = (bf16[128,640]{1,0:T(8,128)(2,1)S(1)}, bf16[128,640]{1,0:T(8,128)(2,1)S(1)}, u32[]{:S(2)}, u32[]{:S(2)}) collective-permute-start(bf16[128,640]{1,0:T(8,128)(2,1)S(1)} %constant_dynamic-slice_fusion), channel_id=1, source_target_pairs={{0,8},{2,10},{4,12},{6,14},{8,0},{10,2},{12,4},{14,6},{1,9},{3,11}... | collective-permute-start | bytes 491528 | tf_op jit(solution)/shard_map/ppermute | solution.py:25
  26.5 0.0 collective-permute-done.6
  26.5 1.2 %collective-permute-start.9 = (bf16[128,640]{1,0:T(8,128)(2,1)S(1)}, bf16[128,640]{1,0:T(8,128)(2,1)S(1)}, u32[]{:S(2)}, u32[]{:S(2)}) collective-permute-start(bf16[128,640]{1,0:T(8,128)(2,1)S(1)} %constant_dynamic-slice_fusion), channel_id=1, source_target_pairs={{0,4},{2,6},{4,0},{6,2},{8,12},{10,14},{12,8},{14,10},{1,5},{3,7},... | collective-permute-start | bytes 491528 | tf_op jit(solution)/shard_map/ppermute | solution.py:25
  27.8 1.0 %collective-permute-start.5 = (bf16[18,8,768]{2,1,0:T(8,128)(2,1)S(1)}, bf16[18,8,768]{2,1,0:T(8,128)(2,1)S(1)}, u32[]{:S(2)}, u32[]{:S(2)}) collective-permute-start(bf16[18,8,768]{2,1,0:T(8,128)(2,1)S(1)} %collective-permute-done.4), channel_id=1, source_target_pairs={{0,2},{2,0},{4,6},{6,4},{8,10},{10,8},{12,14},{14,12},{1,3},{3,1},... | collective-permute-start | bytes 663560 | tf_op jit(solution)/shard_map/ppermute | solution.py:25
  28.7 2.9 %collective-permute-done.7.rest_11_ = bf16[128,640]{1,0:T(8,128)(2,1)S(1)} collective-permute-done((bf16[128,640]{1,0:T(8,128)(2,1)S(1)}, bf16[128,640]{1,0:T(8,128)(2,1)S(1)}, u32[]{:S(2)}, u32[]{:S(2)}) %collective-permute-start.7) | collective-permute-done | bytes 163872 | tf_op jit(solution)/shard_map/ppermute | solution.py:25
  31.7 0.7 %collective-permute-start.8 = (bf16[128,640]{1,0:T(8,128)(2,1)S(1)}, bf16[128,640]{1,0:T(8,128)(2,1)S(1)}, u32[]{:S(2)}, u32[]{:S(2)}) collective-permute-start(bf16[128,640]{1,0:T(8,128)(2,1)S(1)} %collective-permute-done.7.rest_11_), channel_id=1, source_target_pairs={{0,4},{2,6},{4,0},{6,2},{8,12},{10,14},{12,8},{14,10},{1,5},{3,7},... | collective-permute-start | bytes 491528 | tf_op jit(solution)/shard_map/ppermute | solution.py:25
  32.3 0.2 collective-permute-start.11
  32.6 1.8 %collective-permute-done.9.rest_9_ = bf16[128,640]{1,0:T(8,128)(2,1)S(1)} collective-permute-done((bf16[128,640]{1,0:T(8,128)(2,1)S(1)}, bf16[128,640]{1,0:T(8,128)(2,1)S(1)}, u32[]{:S(2)}, u32[]{:S(2)}) %collective-permute-start.9) | collective-permute-done | bytes 163872 | tf_op jit(solution)/shard_map/ppermute | solution.py:25
  34.3 0.0 collective-permute-start.10
  34.4 1.7 %collective-permute-done.5 = bf16[18,8,768]{2,1,0:T(8,128)(2,1)S(1)} collective-permute-done((bf16[18,8,768]{2,1,0:T(8,128)(2,1)S(1)}, bf16[18,8,768]{2,1,0:T(8,128)(2,1)S(1)}, u32[]{:S(2)}, u32[]{:S(2)}) %collective-permute-start.5) | collective-permute-done | bytes 221216 | tf_op jit(solution)/shard_map/ppermute | solution.py:25
  36.1 0.0 copy-done.6
  36.1 0.0 copy-done.7
  36.1 0.0 copy-done.8
  36.1 0.0 copy-start.1
  36.1 0.0 copy-start.2
  36.1 0.0 copy-start.3
  36.1 0.0 copy-start.4
  36.1 0.0 copy-start.5
  36.1 3.3 %tower.1 = (f32[64,768]{1,0:T(8,128)S(1)}, f32[64,768]{1,0:T(8,128)S(1)}, f32[64,768]{1,0:T(8,128)S(1)}, f32[64,768]{1,0:T(8,128)S(1)}) custom-call(s32[128]{0:T(128)S(1)} %copy-done.7, s32[4,16]{1,0:T(4,128)S(1)} %bitcast.18, s32[16]{0:T(128)S(1)} %copy-done.8, bf16[16,768]{1,0:T(8,128)(2,1)S(1)} %constant_dynamic-slice_fusion.2.deltas, ...), custom_call_target="tpu_custom_call" | custom-call | flops 1000000000 | bytes 40000000 | tf_op jit(solution)/shard_map/tower/pallas_call | solution.py:362
  39.4 0.0 collective-permute-done.8.rest_13_
  39.4 0.1 collective-permute-start.12
  39.5 0.5 %collective-permute-start.13 = (f32[64,768]{1,0:T(8,128)S(1)}, f32[64,768]{1,0:T(8,128)S(1)}, u32[]{:S(2)}, u32[]{:S(2)}) collective-permute-start(f32[64,768]{1,0:T(8,128)S(1)} %get-tuple-element.54.rest_1_), channel_id=1, source_target_pairs={{0,1},{1,0},{2,3},{3,2},{4,5},{5,4},{6,7},{7,6},{8,9},{9,8},{10,11... | collective-permute-start | bytes 589832 | tf_op jit(solution)/shard_map/ppermute | solution.py:391
  40.0 0.1 collective-permute-start.14
  40.1 0.0 collective-permute-done.11.rest_12_
  40.1 0.0 collective-permute-done.10.rest_10_
  40.1 0.4 collective-permute-start.15
  40.5 0.9 %collective-permute-start.16 = (bf16[128,640]{1,0:T(8,128)(2,1)S(1)}, bf16[128,640]{1,0:T(8,128)(2,1)S(1)}, u32[]{:S(2)}, u32[]{:S(2)}) collective-permute-start(bf16[128,640]{1,0:T(8,128)(2,1)S(1)} %collective-permute-done.8.rest_13_), channel_id=1, source_target_pairs={{0,2},{2,0},{4,6},{6,4},{8,10},{10,8},{12,14},{14,12},{1,3},{3,1},... | collective-permute-start | bytes 491528 | tf_op jit(solution)/shard_map/ppermute | solution.py:25
  41.4 0.0 collective-permute-done.12.rest_4_
  41.4 0.0 collective-permute-done.13.rest_5_
  41.4 0.1 collective-permute-done.14.rest_6_
  41.5 0.3 collective-permute-done.15.rest_7_
  41.8 0.0 copy-done.1
  41.8 0.0 copy-done.2
  41.8 0.0 copy-done.3
  41.8 0.0 copy-done.4
  41.8 0.0 copy-done.5
  41.8 2.9 %near.1 = (bf16[256,256]{1,0:T(8,128)(2,1)S(1)}, f32[4,256,128]{2,1,0:T(8,128)S(1)}, f32[2,256,256]{2,1,0:T(8,128)S(1)}) custom-call(s32[16]{0:T(128)S(1)} %copy-done.4, f32[2]{0:T(128)S(1)} %copy-done.5, f32[1,1536]{1,0:T(1,128)S(1)} %reshape.6.gain, bf16[1536,256]{1,0:T(8,128)(2,1)S(1)} %copy-done.2, bf16[1536,256]{1,0:T(8,128)(2,1)S(1)} %copy-done.3, ...), custom_call_target="tpu_custom_call" | custom-call | tf_op jit(solution)/shard_map/near/pallas_call | solution.py:397
  44.7 2.0 %collective-permute-done.16.rest_0_ = bf16[128,640]{1,0:T(8,128)(2,1)S(1)} collective-permute-done((bf16[128,640]{1,0:T(8,128)(2,1)S(1)}, bf16[128,640]{1,0:T(8,128)(2,1)S(1)}, u32[]{:S(2)}, u32[]{:S(2)}) %collective-permute-start.16) | collective-permute-done | bytes 163872 | tf_op jit(solution)/shard_map/ppermute | solution.py:25
  46.7 1.8 %far.1 = bf16[256,384]{1,0:T(8,128)(2,1)} custom-call(s32[16]{0:T(128)S(1)} %copy-done.4, f32[2]{0:T(128)S(1)} %copy-done.5, bf16[256,256]{1,0:T(8,128)(2,1)S(1)} %get-tuple-element.62.queries, f32[4,256,128]{2,1,0:T(8,128)S(1)} %get-tuple-element.63.stats, f32[2,256,256]{2,1,0:T(8,128)S(1)} %get-tuple-element.64.sums, ...), custom_call_target="tpu_custom_call" | custom-call | tf_op jit(solution)/shard_map/far/pallas_call | solution.py:419
  (5 shorter events, 0.1 us)
Async XLA Ops:
  0.0 1.0 %copy-start = (bf16[16,8,1536]{2,1,0:T(8,128)(2,1)S(1)}, bf16[16,8,1536]{2,1,0:T(8,128)(2,1)}, u32[]{:S(2)}) copy-start(bf16[16,8,1536]{2,1,0:T(8,128)(2,1)} %param.15) | copy-start | bytes 1179652
  0.0 12.5 %copy-start.10 = (bf16[16,1536]{1,0:T(8,128)(2,1)S(1)}, bf16[16,1536]{1,0:T(8,128)(2,1)}, u32[]{:S(2)}) copy-start(bf16[16,1536]{1,0:T(8,128)(2,1)} %param.21) | copy-start | bytes 147460
  0.0 12.5 %copy-start.9 = (bf16[17,1536]{1,0:T(8,128)(2,1)S(1)}, bf16[17,1536]{1,0:T(8,128)(2,1)}, u32[]{:S(2)}) copy-start(bf16[17,1536]{1,0:T(8,128)(2,1)} %param.22) | copy-start | bytes 156676
  0.0 36.1 %copy-start.6 = (s32[16,4]{0,1:T(4,128)S(1)}, s32[16,4]{0,1:T(4,128)}, u32[]{:S(2)}) copy-start(s32[16,4]{0,1:T(4,128)} %param.18) | copy-start | bytes 772
  0.0 36.1 %copy-start.7 = (s32[128]{0:T(128)S(1)}, s32[128]{0:T(128)}, u32[]{:S(2)}) copy-start(s32[128]{0:T(128)} %block_slot.1) | copy-start | bytes 1540
  0.0 36.0 %copy-start.8 = (s32[16]{0:T(128)S(1)}, s32[16]{0:T(128)}, u32[]{:S(2)}) copy-start(s32[16]{0:T(128)} %window_offsets.1) | copy-start | bytes 196
  1.1 8.9 %collective-permute-start.1 = (bf16[18,8,768]{2,1,0:T(8,128)(2,1)S(1)}, bf16[18,8,768]{2,1,0:T(8,128)(2,1)S(1)}, u32[]{:S(2)}, u32[]{:S(2)}) collective-permute-start(bf16[18,8,768]{2,1,0:T(8,128)(2,1)S(1)} %pack.1), channel_id=1, source_target_pairs={{0,4},{2,6},{4,0},{6,2},{8,12},{10,14},{12,8},{14,10},{1,5},{3,7},... | collective-permute-start | bytes 663560 | tf_op jit(solution)/shard_map/ppermute | solution.py:25
  4.1 6.9 %collective-permute-start.2 = (bf16[18,8,768]{2,1,0:T(8,128)(2,1)S(1)}, bf16[18,8,768]{2,1,0:T(8,128)(2,1)S(1)}, u32[]{:S(2)}, u32[]{:S(2)}) collective-permute-start(bf16[18,8,768]{2,1,0:T(8,128)(2,1)S(1)} %pack.1), channel_id=1, source_target_pairs={{0,2},{2,0},{4,6},{6,4},{8,10},{10,8},{12,14},{14,12},{1,3},{3,1},... | collective-permute-start | bytes 663560 | tf_op jit(solution)/shard_map/ppermute | solution.py:25
  5.6 11.0 %collective-permute-start = (bf16[18,8,768]{2,1,0:T(8,128)(2,1)S(1)}, bf16[18,8,768]{2,1,0:T(8,128)(2,1)S(1)}, u32[]{:S(2)}, u32[]{:S(2)}) collective-permute-start(bf16[18,8,768]{2,1,0:T(8,128)(2,1)S(1)} %pack.1), channel_id=1, source_target_pairs={{0,12},{2,14},{4,8},{6,10},{8,4},{10,6},{12,0},{14,2},{1,13},{3,15... | collective-permute-start | bytes 663560 | tf_op jit(solution)/shard_map/ppermute | solution.py:25
  11.0 7.4 %collective-permute-start.3 = (bf16[18,8,768]{2,1,0:T(8,128)(2,1)S(1)}, bf16[18,8,768]{2,1,0:T(8,128)(2,1)S(1)}, u32[]{:S(2)}, u32[]{:S(2)}) collective-permute-start(bf16[18,8,768]{2,1,0:T(8,128)(2,1)S(1)} %collective-permute-done.1), channel_id=1, source_target_pairs={{0,2},{2,0},{4,6},{6,4},{8,10},{10,8},{12,14},{14,12},{1,3},{3,1},... | collective-permute-start | bytes 663560 | tf_op jit(solution)/shard_map/ppermute | solution.py:25
  16.6 6.2 %collective-permute-start.4 = (bf16[18,8,768]{2,1,0:T(8,128)(2,1)S(1)}, bf16[18,8,768]{2,1,0:T(8,128)(2,1)S(1)}, u32[]{:S(2)}, u32[]{:S(2)}) collective-permute-start(bf16[18,8,768]{2,1,0:T(8,128)(2,1)S(1)} %collective-permute-done), channel_id=1, source_target_pairs={{0,4},{2,6},{4,0},{6,2},{8,12},{10,14},{12,8},{14,10},{1,5},{3,7},... | collective-permute-start | bytes 663560 | tf_op jit(solution)/shard_map/ppermute | solution.py:25
  18.4 8.1 %collective-permute-start.6 = (bf16[18,8,768]{2,1,0:T(8,128)(2,1)S(1)}, bf16[18,8,768]{2,1,0:T(8,128)(2,1)S(1)}, u32[]{:S(2)}, u32[]{:S(2)}) collective-permute-start(bf16[18,8,768]{2,1,0:T(8,128)(2,1)S(1)} %collective-permute-done), channel_id=1, source_target_pairs={{0,2},{2,0},{4,6},{6,4},{8,10},{10,8},{12,14},{14,12},{1,3},{3,1},... | collective-permute-start | bytes 663560 | tf_op jit(solution)/shard_map/ppermute | solution.py:25
  22.8 8.8 %collective-permute-start.7 = (bf16[128,640]{1,0:T(8,128)(2,1)S(1)}, bf16[128,640]{1,0:T(8,128)(2,1)S(1)}, u32[]{:S(2)}, u32[]{:S(2)}) collective-permute-start(bf16[128,640]{1,0:T(8,128)(2,1)S(1)} %constant_dynamic-slice_fusion), channel_id=1, source_target_pairs={{0,8},{2,10},{4,12},{6,14},{8,0},{10,2},{12,4},{14,6},{1,9},{3,11}... | collective-permute-start | bytes 491528 | tf_op jit(solution)/shard_map/ppermute | solution.py:25
  26.5 7.8 %collective-permute-start.9 = (bf16[128,640]{1,0:T(8,128)(2,1)S(1)}, bf16[128,640]{1,0:T(8,128)(2,1)S(1)}, u32[]{:S(2)}, u32[]{:S(2)}) collective-permute-start(bf16[128,640]{1,0:T(8,128)(2,1)S(1)} %constant_dynamic-slice_fusion), channel_id=1, source_target_pairs={{0,4},{2,6},{4,0},{6,2},{8,12},{10,14},{12,8},{14,10},{1,5},{3,7},... | collective-permute-start | bytes 491528 | tf_op jit(solution)/shard_map/ppermute | solution.py:25
  27.8 8.3 %collective-permute-start.5 = (bf16[18,8,768]{2,1,0:T(8,128)(2,1)S(1)}, bf16[18,8,768]{2,1,0:T(8,128)(2,1)S(1)}, u32[]{:S(2)}, u32[]{:S(2)}) collective-permute-start(bf16[18,8,768]{2,1,0:T(8,128)(2,1)S(1)} %collective-permute-done.4), channel_id=1, source_target_pairs={{0,2},{2,0},{4,6},{6,4},{8,10},{10,8},{12,14},{14,12},{1,3},{3,1},... | collective-permute-start | bytes 663560 | tf_op jit(solution)/shard_map/ppermute | solution.py:25
  31.7 7.7 %collective-permute-start.8 = (bf16[128,640]{1,0:T(8,128)(2,1)S(1)}, bf16[128,640]{1,0:T(8,128)(2,1)S(1)}, u32[]{:S(2)}, u32[]{:S(2)}) collective-permute-start(bf16[128,640]{1,0:T(8,128)(2,1)S(1)} %collective-permute-done.7.rest_11_), channel_id=1, source_target_pairs={{0,4},{2,6},{4,0},{6,2},{8,12},{10,14},{12,8},{14,10},{1,5},{3,7},... | collective-permute-start | bytes 491528 | tf_op jit(solution)/shard_map/ppermute | solution.py:25
  32.3 7.7 %collective-permute-start.11 = (bf16[128,640]{1,0:T(8,128)(2,1)S(1)}, bf16[128,640]{1,0:T(8,128)(2,1)S(1)}, u32[]{:S(2)}, u32[]{:S(2)}) collective-permute-start(bf16[128,640]{1,0:T(8,128)(2,1)S(1)} %collective-permute-done.7.rest_11_), channel_id=1, source_target_pairs={{0,2},{2,0},{4,6},{6,4},{8,10},{10,8},{12,14},{14,12},{1,3},{3,1},... | collective-permute-start | bytes 491528 | tf_op jit(solution)/shard_map/ppermute | solution.py:25
  34.3 5.7 %collective-permute-start.10 = (bf16[128,640]{1,0:T(8,128)(2,1)S(1)}, bf16[128,640]{1,0:T(8,128)(2,1)S(1)}, u32[]{:S(2)}, u32[]{:S(2)}) collective-permute-start(bf16[128,640]{1,0:T(8,128)(2,1)S(1)} %collective-permute-done.9.rest_9_), channel_id=1, source_target_pairs={{0,2},{2,0},{4,6},{6,4},{8,10},{10,8},{12,14},{14,12},{1,3},{3,1},... | collective-permute-start | bytes 491528 | tf_op jit(solution)/shard_map/ppermute | solution.py:25
  36.1 5.7 %copy-start.1 = (bf16[1536,384]{1,0:T(8,128)(2,1)S(1)}, bf16[1536,384]{1,0:T(8,128)(2,1)}, u32[]{:S(2)}) copy-start(bf16[1536,384]{1,0:T(8,128)(2,1)} %w_value.1) | copy-start | bytes 3538948
  36.1 5.7 %copy-start.2 = (bf16[1536,256]{1,0:T(8,128)(2,1)S(1)}, bf16[1536,256]{1,0:T(8,128)(2,1)}, u32[]{:S(2)}) copy-start(bf16[1536,256]{1,0:T(8,128)(2,1)} %w_query.1) | copy-start | bytes 2359300
  36.1 5.7 %copy-start.3 = (bf16[1536,256]{1,0:T(8,128)(2,1)S(1)}, bf16[1536,256]{1,0:T(8,128)(2,1)}, u32[]{:S(2)}) copy-start(bf16[1536,256]{1,0:T(8,128)(2,1)} %w_key.1) | copy-start | bytes 2359300
  36.1 5.7 %copy-start.4 = (s32[16]{0:T(128)S(1)}, s32[16]{0:T(128)}, u32[]{:S(2)}) copy-start(s32[16]{0:T(128)} %positions.3) | copy-start | bytes 196
  36.1 5.7 %copy-start.5 = (f32[2]{0:T(128)S(1)}, f32[2]{0:T(128)}, u32[]{:S(2)}) copy-start(f32[2]{0:T(128)} %slopes.3) | copy-start | bytes 28
  39.4 2.0 %collective-permute-start.12 = (f32[64,768]{1,0:T(8,128)S(1)}, f32[64,768]{1,0:T(8,128)S(1)}, u32[]{:S(2)}, u32[]{:S(2)}) collective-permute-start(f32[64,768]{1,0:T(8,128)S(1)} %get-tuple-element.53.rest_0_), channel_id=1, source_target_pairs={{0,1},{1,0},{2,3},{3,2},{4,5},{5,4},{6,7},{7,6},{8,9},{9,8},{10,11... | collective-permute-start | bytes 589832 | tf_op jit(solution)/shard_map/ppermute | solution.py:391
  39.5 1.9 %collective-permute-start.13 = (f32[64,768]{1,0:T(8,128)S(1)}, f32[64,768]{1,0:T(8,128)S(1)}, u32[]{:S(2)}, u32[]{:S(2)}) collective-permute-start(f32[64,768]{1,0:T(8,128)S(1)} %get-tuple-element.54.rest_1_), channel_id=1, source_target_pairs={{0,1},{1,0},{2,3},{3,2},{4,5},{5,4},{6,7},{7,6},{8,9},{9,8},{10,11... | collective-permute-start | bytes 589832 | tf_op jit(solution)/shard_map/ppermute | solution.py:391
  40.0 1.5 %collective-permute-start.14 = (f32[64,768]{1,0:T(8,128)S(1)}, f32[64,768]{1,0:T(8,128)S(1)}, u32[]{:S(2)}, u32[]{:S(2)}) collective-permute-start(f32[64,768]{1,0:T(8,128)S(1)} %get-tuple-element.55.rest_2_), channel_id=1, source_target_pairs={{0,1},{1,0},{2,3},{3,2},{4,5},{5,4},{6,7},{7,6},{8,9},{9,8},{10,11... | collective-permute-start | bytes 589832 | tf_op jit(solution)/shard_map/ppermute | solution.py:391
  40.1 1.7 %collective-permute-start.15 = (f32[64,768]{1,0:T(8,128)S(1)}, f32[64,768]{1,0:T(8,128)S(1)}, u32[]{:S(2)}, u32[]{:S(2)}) collective-permute-start(f32[64,768]{1,0:T(8,128)S(1)} %get-tuple-element.58.rest_3_), channel_id=1, source_target_pairs={{0,1},{1,0},{2,3},{3,2},{4,5},{5,4},{6,7},{7,6},{8,9},{9,8},{10,11... | collective-permute-start | bytes 589832 | tf_op jit(solution)/shard_map/ppermute | solution.py:391
  40.5 6.2 %collective-permute-start.16 = (bf16[128,640]{1,0:T(8,128)(2,1)S(1)}, bf16[128,640]{1,0:T(8,128)(2,1)S(1)}, u32[]{:S(2)}, u32[]{:S(2)}) collective-permute-start(bf16[128,640]{1,0:T(8,128)(2,1)S(1)} %collective-permute-done.8.rest_13_), channel_id=1, source_target_pairs={{0,2},{2,0},{4,6},{6,4},{8,10},{10,8},{12,14},{14,12},{1,3},{3,1},... | collective-permute-start | bytes 491528 | tf_op jit(solution)/shard_map/ppermute | solution.py:25

commit v2 on v1

--- a/solution.py
+++ b/solution.py
@@ -12,7 +12,7 @@
 RADIUS = 8
 TAPS = 2 * RADIUS + 1
 EPSILON = 1e-06
-PARTS = 4
+PARTS = 3
 
 
 def send(x, seq_mask, var_mask=0):
@@ -57,23 +57,13 @@
     cells_3, across_1 = then(cells_3, across_1)
     across_3 = send(cells_3, 0, 1)
     cells_2, share = then(cells_2, share)
-    across_2, share_2 = send(cells_2, 0, 1), send(share, 2)
-    across_3, share = then(across_3, share)
-    share_1 = send(share, 1)
-    share_3 = send(share_2, 1)
-    share_across_2, share_across_1 = send(share_2, 0, 1), send(share_1, 0, 1)
-    share_across_3 = send(share_3, 0, 1)
+    across_2, share_3 = send(cells_2, 0, 1), send(share, 3)
+    across_3, share_3, window = then(across_3, share_3, window)
+    share_2, share_across_3 = send(share_3, 1), send(share_3, 0, 1)
+    window_1, share_across_2 = send(window, 1), send(share_2, 0, 1)
 
     pieces = [cells, across, cells_1, across_1, cells_2, across_2, cells_3, across_3]
-    windows = [
-        window,
-        share_1,
-        share_across_1,
-        share_2,
-        share_across_2,
-        share_3,
-        share_across_3,
-    ]
+    windows = [window, window_1, share_3, share_across_3, share_2, share_across_2]
     return [piece[None] for piece in pieces], windows, small
 
 
@@ -93,8 +83,8 @@
     me_seq, me_var = lax.axis_index("seq"), lax.axis_index("var")
     if not on_line(seq, var):
         return [[rows * p for p in range(seq)]]
-    firsts = [[me_seq * rows]]
-    for mask in (1, 2, 3):
+    firsts = [[me_seq * rows], [(me_seq ^ 1) * rows]]
+    for mask in (3, 2):
         for side in (0, 1):
             firsts.append([(me_seq ^ mask) * rows + (me_var ^ side) * (rows // 2)])
     return firsts
@@ -384,9 +374,9 @@
     )
     swap = [(0, 1), (1, 0)]
     if len(window_pieces) > 2:
-        *towers, window_pieces[5] = then(*towers, window_pieces[5])
+        *towers, window_pieces[4] = then(*towers, window_pieces[4])
         *towers, last = towers
-        last, window_pieces[2], window_pieces[4] = then(last, window_pieces[2], window_pieces[4])
+        last, window_pieces[3] = then(last, window_pieces[3])
         towers = [*towers, last]
     others = [lax.ppermute(tower, "rep", swap) for tower in towers]
     heads, rows = head_slopes.shape[0], variants * W

time: 49.4 us -> 47.4 us (0.960); the launches traced: 48.5 us -> 47.3 us
  waiting for transfers between devices: 17.9 us -> 15.9 us
  starting transfers between devices: 19.7 us -> 21.1 us
  local copies, waits for them, and re-layouts: 1.77 us -> 1.07 us
    ppermute x13 -> x12, starting transfers between devices: 18.6 us -> 20.5 us  [send(): return lax.ppermute(x, ('seq', 'var'), pairs)]
    ppermute x13 -> x12, waiting for transfers between devices: 17.6 us -> 15.9 us  [send(): return lax.ppermute(x, ('seq', 'var'), pairs)]
    reshape x1, local copies, waits for them, and re-layouts: 0.7 us -> 0.01 us  [on_device(): norm_gain.reshape(1, channels)]
    ppermute x4 -> x3, starting transfers between devices: 1.08 us -> 0.65 us  [on_device(): others = [lax.ppermute(tower, 'rep', swap) for tower in towers]]
  transfers between devices with their start and end apart: 17 -> 15, of which waited for: 10 -> 8; matrix products, arithmetic and copies ran while one was open for 4% -> 2% of each run, Pallas kernels for 13% -> 13%
where the time goes in v2:
time: 47.4 us; the launch traced here: 47.3 us
  starting transfers between devices  21.1 us (45%)
  waiting for transfers between devices  15.9 us (34%)
  Pallas kernels  7.86 us (17%)
  local copies, waits for them, and re-layouts  1.07 us (2%)
  other arithmetic  1.03 us (2%)
    ppermute x12, starting transfers between devices, send(): return lax.ppermute(x, ('seq', 'var'), pairs)  20.5 us
    ppermute x12, waiting for transfers between devices, send(): return lax.ppermute(x, ('seq', 'var'), pairs)  15.9 us
    pallas_call x1, Pallas kernels, on_device(): pl.pallas_call(functools.partial(tower_kernel, per_owner), out_shape=towe...  3.25 us
    pallas_call x1, Pallas kernels, on_device(): pl.pallas_call(functools.partial(near_kernel, sizes), out_shape=[jax.Shap...  2.76 us
    pallas_call x1, Pallas kernels, on_device(): pl.pallas_call(functools.partial(far_kernel, sizes), out_shape=jax.ShapeD...  1.83 us
    concatenate x1, other arithmetic, on_device(): window = jnp.concatenate([ref_keys, ref_values], axis=1)  1.03 us
  transfers between devices with their start and end apart: 15, of which 8 were waited for; matrix products, arithmetic and copies ran while one was open for 2% of the time, Pallas kernels for 13%

profile of v2, /device:TPU:0, one launch (start us, length us, event | category | flops | bytes accessed | tf_op | source)
XLA Modules:
  0.0 47.3 jit_solution(18024969292260503354)
XLA Ops:
  0.0 0.0 copy-start
  0.0 0.0 copy-start.10
  0.0 0.0 copy-start.11
  0.0 0.0 copy-start.9
  0.0 0.0 copy-start.6
  0.0 0.0 copy-start.7
  0.0 0.0 copy-start.8
  0.0 0.8 %constant_dynamic-slice_fusion.4.scales = bf16[16,768]{1,0:T(8,128)(2,1)S(1)} fusion(bf16[16,1536]{1,0:T(8,128)(2,1)} %param.16, s32[]{:T(128)S(6)} %select_n.4), kind=kLoop, calls=%fused_computation.5 | loop fusion | bytes 49156 | tf_op jit(solution)/shard_map/dynamic_slice | solution.py:326
  0.8 0.2 copy-done
  1.1 3.1 %collective-permute-start.1 = (bf16[18,8,768]{2,1,0:T(8,128)(2,1)S(1)}, bf16[18,8,768]{2,1,0:T(8,128)(2,1)S(1)}, u32[]{:S(2)}, u32[]{:S(2)}) collective-permute-start(bf16[18,8,768]{2,1,0:T(8,128)(2,1)S(1)} %pack.1), channel_id=1, source_target_pairs={{0,4},{2,6},{4,0},{6,2},{8,12},{10,14},{12,8},{14,10},{1,5},{3,7},... | collective-permute-start | bytes 663560 | tf_op jit(solution)/shard_map/ppermute | solution.py:25
  4.1 1.5 %collective-permute-start.2 = (bf16[18,8,768]{2,1,0:T(8,128)(2,1)S(1)}, bf16[18,8,768]{2,1,0:T(8,128)(2,1)S(1)}, u32[]{:S(2)}, u32[]{:S(2)}) collective-permute-start(bf16[18,8,768]{2,1,0:T(8,128)(2,1)S(1)} %pack.1), channel_id=1, source_target_pairs={{0,2},{2,0},{4,6},{6,4},{8,10},{10,8},{12,14},{14,12},{1,3},{3,1},... | collective-permute-start | bytes 663560 | tf_op jit(solution)/shard_map/ppermute | solution.py:25
  5.6 2.5 %collective-permute-start = (bf16[18,8,768]{2,1,0:T(8,128)(2,1)S(1)}, bf16[18,8,768]{2,1,0:T(8,128)(2,1)S(1)}, u32[]{:S(2)}, u32[]{:S(2)}) collective-permute-start(bf16[18,8,768]{2,1,0:T(8,128)(2,1)S(1)} %pack.1), channel_id=1, source_target_pairs={{0,12},{2,14},{4,8},{6,10},{8,4},{10,6},{12,0},{14,2},{1,13},{3,15... | collective-permute-start | bytes 663560 | tf_op jit(solution)/shard_map/ppermute | solution.py:25
  8.1 1.0 %pad_maximum_fusion.rest_6_ = bf16[256,640]{1,0:T(8,128)(2,1)S(1)} fusion(bf16[256,384]{1,0:T(8,128)(2,1)} %param.28, bf16[256,256]{1,0:T(8,128)(2,1)} %param.27), kind=kLoop, calls=%fused_computation | loop fusion | flops 655360 | bytes 655360 | tf_op jit(solution)/shard_map/concatenate | solution.py:338
  9.1 0.8 %collective-permute-done.1 = bf16[18,8,768]{2,1,0:T(8,128)(2,1)S(1)} collective-permute-done((bf16[18,8,768]{2,1,0:T(8,128)(2,1)S(1)}, bf16[18,8,768]{2,1,0:T(8,128)(2,1)S(1)}, u32[]{:S(2)}, u32[]{:S(2)}) %collective-permute-start.1) | collective-permute-done | bytes 221216 | tf_op jit(solution)/shard_map/ppermute | solution.py:25
  10.0 1.1 %collective-permute-done.2 = bf16[18,8,768]{2,1,0:T(8,128)(2,1)S(1)} collective-permute-done((bf16[18,8,768]{2,1,0:T(8,128)(2,1)S(1)}, bf16[18,8,768]{2,1,0:T(8,128)(2,1)S(1)}, u32[]{:S(2)}, u32[]{:S(2)}) %collective-permute-start.2) | collective-permute-done | bytes 221216 | tf_op jit(solution)/shard_map/ppermute | solution.py:25
  11.0 1.5 %collective-permute-start.3 = (bf16[18,8,768]{2,1,0:T(8,128)(2,1)S(1)}, bf16[18,8,768]{2,1,0:T(8,128)(2,1)S(1)}, u32[]{:S(2)}, u32[]{:S(2)}) collective-permute-start(bf16[18,8,768]{2,1,0:T(8,128)(2,1)S(1)} %collective-permute-done.1), channel_id=1, source_target_pairs={{0,2},{2,0},{4,6},{6,4},{8,10},{10,8},{12,14},{14,12},{1,3},{3,1},... | collective-permute-start | bytes 663560 | tf_op jit(solution)/shard_map/ppermute | solution.py:25
  12.5 0.0 copy-done.10
  12.5 0.0 copy-done.11
  12.5 0.0 copy-done.9
  12.6 4.0 %collective-permute-done = bf16[18,8,768]{2,1,0:T(8,128)(2,1)S(1)} collective-permute-done((bf16[18,8,768]{2,1,0:T(8,128)(2,1)S(1)}, bf16[18,8,768]{2,1,0:T(8,128)(2,1)S(1)}, u32[]{:S(2)}, u32[]{:S(2)}) %collective-permute-start) | collective-permute-done | bytes 221216 | tf_op jit(solution)/shard_map/ppermute | solution.py:25
  16.6 1.8 %collective-permute-start.4 = (bf16[18,8,768]{2,1,0:T(8,128)(2,1)S(1)}, bf16[18,8,768]{2,1,0:T(8,128)(2,1)S(1)}, u32[]{:S(2)}, u32[]{:S(2)}) collective-permute-start(bf16[18,8,768]{2,1,0:T(8,128)(2,1)S(1)} %collective-permute-done), channel_id=1, source_target_pairs={{0,4},{2,6},{4,0},{6,2},{8,12},{10,14},{12,8},{14,10},{1,5},{3,7},... | collective-permute-start | bytes 663560 | tf_op jit(solution)/shard_map/ppermute | solution.py:25
  18.4 0.0 collective-permute-done.3
  18.4 0.5 %collective-permute-start.6 = (bf16[18,8,768]{2,1,0:T(8,128)(2,1)S(1)}, bf16[18,8,768]{2,1,0:T(8,128)(2,1)S(1)}, u32[]{:S(2)}, u32[]{:S(2)}) collective-permute-start(bf16[18,8,768]{2,1,0:T(8,128)(2,1)S(1)} %collective-permute-done), channel_id=1, source_target_pairs={{0,2},{2,0},{4,6},{6,4},{8,10},{10,8},{12,14},{14,12},{1,3},{3,1},... | collective-permute-start | bytes 663560 | tf_op jit(solution)/shard_map/ppermute | solution.py:25
  19.0 3.9 %collective-permute-done.4 = bf16[18,8,768]{2,1,0:T(8,128)(2,1)S(1)} collective-permute-done((bf16[18,8,768]{2,1,0:T(8,128)(2,1)S(1)}, bf16[18,8,768]{2,1,0:T(8,128)(2,1)S(1)}, u32[]{:S(2)}, u32[]{:S(2)}) %collective-permute-start.4) | collective-permute-done | bytes 221216 | tf_op jit(solution)/shard_map/ppermute | solution.py:25
  22.8 4.3 %collective-permute-start.7 = (bf16[128,640]{1,0:T(8,128)(2,1)S(1)}, bf16[128,640]{1,0:T(8,128)(2,1)S(1)}, u32[]{:S(2)}, u32[]{:S(2)}) collective-permute-start(bf16[128,640]{1,0:T(8,128)(2,1)S(1)} %constant_dynamic-slice_fusion), channel_id=1, source_target_pairs={{0,12},{2,14},{4,8},{6,10},{8,4},{10,6},{12,0},{14,2},{1,13},{3,15... | collective-permute-start | bytes 491528 | tf_op jit(solution)/shard_map/ppermute | solution.py:25
  27.2 1.0 %collective-permute-start.5 = (bf16[18,8,768]{2,1,0:T(8,128)(2,1)S(1)}, bf16[18,8,768]{2,1,0:T(8,128)(2,1)S(1)}, u32[]{:S(2)}, u32[]{:S(2)}) collective-permute-start(bf16[18,8,768]{2,1,0:T(8,128)(2,1)S(1)} %collective-permute-done.4), channel_id=1, source_target_pairs={{0,2},{2,0},{4,6},{6,4},{8,10},{10,8},{12,14},{14,12},{1,3},{3,1},... | collective-permute-start | bytes 663560 | tf_op jit(solution)/shard_map/ppermute | solution.py:25
  28.2 3.0 %collective-permute-done.7.rest_8_ = bf16[128,640]{1,0:T(8,128)(2,1)S(1)} collective-permute-done((bf16[128,640]{1,0:T(8,128)(2,1)S(1)}, bf16[128,640]{1,0:T(8,128)(2,1)S(1)}, u32[]{:S(2)}, u32[]{:S(2)}) %collective-permute-start.7) | collective-permute-done | bytes 163872 | tf_op jit(solution)/shard_map/ppermute | solution.py:25
  31.1 0.0 collective-permute-done.6
  31.2 0.7 %collective-permute-start.8 = (bf16[128,640]{1,0:T(8,128)(2,1)S(1)}, bf16[128,640]{1,0:T(8,128)(2,1)S(1)}, u32[]{:S(2)}, u32[]{:S(2)}) collective-permute-start(bf16[128,640]{1,0:T(8,128)(2,1)S(1)} %collective-permute-done.7.rest_8_), channel_id=1, source_target_pairs={{0,4},{2,6},{4,0},{6,2},{8,12},{10,14},{12,8},{14,10},{1,5},{3,7},... | collective-permute-start | bytes 491528 | tf_op jit(solution)/shard_map/ppermute | solution.py:25
  31.8 0.9 %collective-permute-start.9 = (bf16[128,640]{1,0:T(8,128)(2,1)S(1)}, bf16[128,640]{1,0:T(8,128)(2,1)S(1)}, u32[]{:S(2)}, u32[]{:S(2)}) collective-permute-start(bf16[128,640]{1,0:T(8,128)(2,1)S(1)} %collective-permute-done.7.rest_8_), channel_id=1, source_target_pairs={{0,2},{2,0},{4,6},{6,4},{8,10},{10,8},{12,14},{14,12},{1,3},{3,1},... | collective-permute-start | bytes 491528 | tf_op jit(solution)/shard_map/ppermute | solution.py:25
  32.7 2.0 %collective-permute-start.13 = (bf16[256,640]{1,0:T(8,128)(2,1)S(1)}, bf16[256,640]{1,0:T(8,128)(2,1)S(1)}, u32[]{:S(2)}, u32[]{:S(2)}) collective-permute-start(bf16[256,640]{1,0:T(8,128)(2,1)S(1)} %pad_maximum_fusion.rest_6_), channel_id=1, source_target_pairs={{0,4},{2,6},{4,0},{6,2},{8,12},{10,14},{12,8},{14,10},{1,5},{3,7},... | collective-permute-start | bytes 983048 | tf_op jit(solution)/shard_map/ppermute | solution.py:25
  34.8 0.1 collective-permute-done.5
  34.9 0.0 copy-done.6
  34.9 0.0 copy-done.7
  34.9 0.0 copy-done.8
  34.9 0.0 copy-start.1
  34.9 0.0 copy-start.2
  34.9 0.0 copy-start.3
  34.9 0.0 copy-start.4
  34.9 0.0 copy-start.5
  34.9 3.3 %tower.1 = (f32[96,768]{1,0:T(8,128)S(1)}, f32[80,768]{1,0:T(8,128)S(1)}, f32[80,768]{1,0:T(8,128)S(1)}) custom-call(s32[128]{0:T(128)S(1)} %copy-done.7, s32[4,16]{1,0:T(4,128)S(1)} %bitcast.18, s32[16]{0:T(128)S(1)} %copy-done.8, bf16[16,768]{1,0:T(8,128)(2,1)S(1)} %constant_dynamic-slice_fusion.2.deltas, ...), custom_call_target="tpu_custom_call" | custom-call | flops 1000000000 | bytes 40000000 | tf_op jit(solution)/shard_map/tower/pallas_call | solution.py:352
  38.2 0.0 collective-permute-done.8.rest_10_
  38.2 0.1 collective-permute-start.10
  38.3 0.0 collective-permute-done.9.rest_9_
  38.3 0.5 %collective-permute-start.12 = (f32[80,768]{1,0:T(8,128)S(1)}, f32[80,768]{1,0:T(8,128)S(1)}, u32[]{:S(2)}, u32[]{:S(2)}) collective-permute-start(f32[80,768]{1,0:T(8,128)S(1)} %get-tuple-element.54.rest_2_), channel_id=1, source_target_pairs={{0,1},{1,0},{2,3},{3,2},{4,5},{5,4},{6,7},{7,6},{8,9},{9,8},{10,11... | collective-permute-start | bytes 737288 | tf_op jit(solution)/shard_map/ppermute | solution.py:381
  38.8 0.1 collective-permute-start.11
  38.9 0.7 %collective-permute-start.14 = (bf16[128,640]{1,0:T(8,128)(2,1)S(1)}, bf16[128,640]{1,0:T(8,128)(2,1)S(1)}, u32[]{:S(2)}, u32[]{:S(2)}) collective-permute-start(bf16[128,640]{1,0:T(8,128)(2,1)S(1)} %collective-permute-done.8.rest_10_), channel_id=1, source_target_pairs={{0,2},{2,0},{4,6},{6,4},{8,10},{10,8},{12,14},{14,12},{1,3},{3,1},... | collective-permute-start | bytes 491528 | tf_op jit(solution)/shard_map/ppermute | solution.py:25
  39.6 1.6 %collective-permute-done.13.rest_7_ = bf16[256,640]{1,0:T(8,128)(2,1)S(1)} collective-permute-done((bf16[256,640]{1,0:T(8,128)(2,1)S(1)}, bf16[256,640]{1,0:T(8,128)(2,1)S(1)}, u32[]{:S(2)}, u32[]{:S(2)}) %collective-permute-start.13) | collective-permute-done | bytes 327712 | tf_op jit(solution)/shard_map/ppermute | solution.py:25
  41.1 0.0 collective-permute-done.12.rest_5_
  41.1 0.0 collective-permute-done.11.rest_4_
  41.1 0.0 collective-permute-done.10.rest_3_
  41.1 0.0 copy-done.1
  41.1 0.0 copy-done.2
  41.1 0.0 copy-done.3
  41.2 0.0 copy-done.4
  41.2 0.0 copy-done.5
  41.2 2.8 %near.1 = (bf16[256,256]{1,0:T(8,128)(2,1)S(1)}, f32[4,256,128]{2,1,0:T(8,128)S(1)}, f32[2,256,256]{2,1,0:T(8,128)S(1)}) custom-call(s32[16]{0:T(128)S(1)} %copy-done.4, f32[2]{0:T(128)S(1)} %copy-done.5, f32[1,1536]{1,0:T(1,128)S(1)} %reshape.6.gain, bf16[1536,256]{1,0:T(8,128)(2,1)S(1)} %copy-done.2, bf16[1536,256]{1,0:T(8,128)(2,1)S(1)} %copy-done.3, ...), custom_call_target="tpu_custom_call" | custom-call | tf_op jit(solution)/shard_map/near/pallas_call | solution.py:387
  43.9 1.5 %collective-permute-done.14.rest_0_ = bf16[128,640]{1,0:T(8,128)(2,1)S(1)} collective-permute-done((bf16[128,640]{1,0:T(8,128)(2,1)S(1)}, bf16[128,640]{1,0:T(8,128)(2,1)S(1)}, u32[]{:S(2)}, u32[]{:S(2)}) %collective-permute-start.14) | collective-permute-done | bytes 163872 | tf_op jit(solution)/shard_map/ppermute | solution.py:25
  45.4 1.8 %far.1 = bf16[256,384]{1,0:T(8,128)(2,1)} custom-call(s32[16]{0:T(128)S(1)} %copy-done.4, f32[2]{0:T(128)S(1)} %copy-done.5, bf16[256,256]{1,0:T(8,128)(2,1)S(1)} %get-tuple-element.58.queries, f32[4,256,128]{2,1,0:T(8,128)S(1)} %get-tuple-element.59.stats, f32[2,256,256]{2,1,0:T(8,128)S(1)} %get-tuple-element.60.sums, ...), custom_call_target="tpu_custom_call" | custom-call | tf_op jit(solution)/shard_map/far/pallas_call | solution.py:409
  (6 shorter events, 0.1 us)
Async XLA Ops:
  0.0 1.0 %copy-start = (bf16[16,8,1536]{2,1,0:T(8,128)(2,1)S(1)}, bf16[16,8,1536]{2,1,0:T(8,128)(2,1)}, u32[]{:S(2)}) copy-start(bf16[16,8,1536]{2,1,0:T(8,128)(2,1)} %param.15) | copy-start | bytes 1179652
  0.0 12.5 %copy-start.10 = (bf16[16,1536]{1,0:T(8,128)(2,1)S(1)}, bf16[16,1536]{1,0:T(8,128)(2,1)}, u32[]{:S(2)}) copy-start(bf16[16,1536]{1,0:T(8,128)(2,1)} %param.21) | copy-start | bytes 147460
  0.0 12.5 %copy-start.11 = (f32[1536]{0:T(1024)S(1)}, f32[1536]{0:T(1024)}, u32[]{:S(2)}) copy-start(f32[1536]{0:T(1024)} %param.23) | copy-start | bytes 18436
  0.0 12.5 %copy-start.9 = (bf16[17,1536]{1,0:T(8,128)(2,1)S(1)}, bf16[17,1536]{1,0:T(8,128)(2,1)}, u32[]{:S(2)}) copy-start(bf16[17,1536]{1,0:T(8,128)(2,1)} %param.22) | copy-start | bytes 156676
  0.0 34.9 %copy-start.6 = (s32[16,4]{0,1:T(4,128)S(1)}, s32[16,4]{0,1:T(4,128)}, u32[]{:S(2)}) copy-start(s32[16,4]{0,1:T(4,128)} %param.18) | copy-start | bytes 772
  0.0 34.9 %copy-start.7 = (s32[128]{0:T(128)S(1)}, s32[128]{0:T(128)}, u32[]{:S(2)}) copy-start(s32[128]{0:T(128)} %block_slot.1) | copy-start | bytes 1540
  0.0 34.8 %copy-start.8 = (s32[16]{0:T(128)S(1)}, s32[16]{0:T(128)}, u32[]{:S(2)}) copy-start(s32[16]{0:T(128)} %window_offsets.1) | copy-start | bytes 196
  1.1 8.9 %collective-permute-start.1 = (bf16[18,8,768]{2,1,0:T(8,128)(2,1)S(1)}, bf16[18,8,768]{2,1,0:T(8,128)(2,1)S(1)}, u32[]{:S(2)}, u32[]{:S(2)}) collective-permute-start(bf16[18,8,768]{2,1,0:T(8,128)(2,1)S(1)} %pack.1), channel_id=1, source_target_pairs={{0,4},{2,6},{4,0},{6,2},{8,12},{10,14},{12,8},{14,10},{1,5},{3,7},... | collective-permute-start | bytes 663560 | tf_op jit(solution)/shard_map/ppermute | solution.py:25
  4.1 6.9 %collective-permute-start.2 = (bf16[18,8,768]{2,1,0:T(8,128)(2,1)S(1)}, bf16[18,8,768]{2,1,0:T(8,128)(2,1)S(1)}, u32[]{:S(2)}, u32[]{:S(2)}) collective-permute-start(bf16[18,8,768]{2,1,0:T(8,128)(2,1)S(1)} %pack.1), channel_id=1, source_target_pairs={{0,2},{2,0},{4,6},{6,4},{8,10},{10,8},{12,14},{14,12},{1,3},{3,1},... | collective-permute-start | bytes 663560 | tf_op jit(solution)/shard_map/ppermute | solution.py:25
  5.6 11.0 %collective-permute-start = (bf16[18,8,768]{2,1,0:T(8,128)(2,1)S(1)}, bf16[18,8,768]{2,1,0:T(8,128)(2,1)S(1)}, u32[]{:S(2)}, u32[]{:S(2)}) collective-permute-start(bf16[18,8,768]{2,1,0:T(8,128)(2,1)S(1)} %pack.1), channel_id=1, source_target_pairs={{0,12},{2,14},{4,8},{6,10},{8,4},{10,6},{12,0},{14,2},{1,13},{3,15... | collective-permute-start | bytes 663560 | tf_op jit(solution)/shard_map/ppermute | solution.py:25
  11.0 7.4 %collective-permute-start.3 = (bf16[18,8,768]{2,1,0:T(8,128)(2,1)S(1)}, bf16[18,8,768]{2,1,0:T(8,128)(2,1)S(1)}, u32[]{:S(2)}, u32[]{:S(2)}) collective-permute-start(bf16[18,8,768]{2,1,0:T(8,128)(2,1)S(1)} %collective-permute-done.1), channel_id=1, source_target_pairs={{0,2},{2,0},{4,6},{6,4},{8,10},{10,8},{12,14},{14,12},{1,3},{3,1},... | collective-permute-start | bytes 663560 | tf_op jit(solution)/shard_map/ppermute | solution.py:25
  16.6 6.2 %collective-permute-start.4 = (bf16[18,8,768]{2,1,0:T(8,128)(2,1)S(1)}, bf16[18,8,768]{2,1,0:T(8,128)(2,1)S(1)}, u32[]{:S(2)}, u32[]{:S(2)}) collective-permute-start(bf16[18,8,768]{2,1,0:T(8,128)(2,1)S(1)} %collective-permute-done), channel_id=1, source_target_pairs={{0,4},{2,6},{4,0},{6,2},{8,12},{10,14},{12,8},{14,10},{1,5},{3,7},... | collective-permute-start | bytes 663560 | tf_op jit(solution)/shard_map/ppermute | solution.py:25
  18.4 12.8 %collective-permute-start.6 = (bf16[18,8,768]{2,1,0:T(8,128)(2,1)S(1)}, bf16[18,8,768]{2,1,0:T(8,128)(2,1)S(1)}, u32[]{:S(2)}, u32[]{:S(2)}) collective-permute-start(bf16[18,8,768]{2,1,0:T(8,128)(2,1)S(1)} %collective-permute-done), channel_id=1, source_target_pairs={{0,2},{2,0},{4,6},{6,4},{8,10},{10,8},{12,14},{14,12},{1,3},{3,1},... | collective-permute-start | bytes 663560 | tf_op jit(solution)/shard_map/ppermute | solution.py:25
  22.8 8.3 %collective-permute-start.7 = (bf16[128,640]{1,0:T(8,128)(2,1)S(1)}, bf16[128,640]{1,0:T(8,128)(2,1)S(1)}, u32[]{:S(2)}, u32[]{:S(2)}) collective-permute-start(bf16[128,640]{1,0:T(8,128)(2,1)S(1)} %constant_dynamic-slice_fusion), channel_id=1, source_target_pairs={{0,12},{2,14},{4,8},{6,10},{8,4},{10,6},{12,0},{14,2},{1,13},{3,15... | collective-permute-start | bytes 491528 | tf_op jit(solution)/shard_map/ppermute | solution.py:25
  27.2 7.7 %collective-permute-start.5 = (bf16[18,8,768]{2,1,0:T(8,128)(2,1)S(1)}, bf16[18,8,768]{2,1,0:T(8,128)(2,1)S(1)}, u32[]{:S(2)}, u32[]{:S(2)}) collective-permute-start(bf16[18,8,768]{2,1,0:T(8,128)(2,1)S(1)} %collective-permute-done.4), channel_id=1, source_target_pairs={{0,2},{2,0},{4,6},{6,4},{8,10},{10,8},{12,14},{14,12},{1,3},{3,1},... | collective-permute-start | bytes 663560 | tf_op jit(solution)/shard_map/ppermute | solution.py:25
  31.2 7.1 %collective-permute-start.8 = (bf16[128,640]{1,0:T(8,128)(2,1)S(1)}, bf16[128,640]{1,0:T(8,128)(2,1)S(1)}, u32[]{:S(2)}, u32[]{:S(2)}) collective-permute-start(bf16[128,640]{1,0:T(8,128)(2,1)S(1)} %collective-permute-done.7.rest_8_), channel_id=1, source_target_pairs={{0,4},{2,6},{4,0},{6,2},{8,12},{10,14},{12,8},{14,10},{1,5},{3,7},... | collective-permute-start | bytes 491528 | tf_op jit(solution)/shard_map/ppermute | solution.py:25
  31.8 6.4 %collective-permute-start.9 = (bf16[128,640]{1,0:T(8,128)(2,1)S(1)}, bf16[128,640]{1,0:T(8,128)(2,1)S(1)}, u32[]{:S(2)}, u32[]{:S(2)}) collective-permute-start(bf16[128,640]{1,0:T(8,128)(2,1)S(1)} %collective-permute-done.7.rest_8_), channel_id=1, source_target_pairs={{0,2},{2,0},{4,6},{6,4},{8,10},{10,8},{12,14},{14,12},{1,3},{3,1},... | collective-permute-start | bytes 491528 | tf_op jit(solution)/shard_map/ppermute | solution.py:25
  32.7 8.4 %collective-permute-start.13 = (bf16[256,640]{1,0:T(8,128)(2,1)S(1)}, bf16[256,640]{1,0:T(8,128)(2,1)S(1)}, u32[]{:S(2)}, u32[]{:S(2)}) collective-permute-start(bf16[256,640]{1,0:T(8,128)(2,1)S(1)} %pad_maximum_fusion.rest_6_), channel_id=1, source_target_pairs={{0,4},{2,6},{4,0},{6,2},{8,12},{10,14},{12,8},{14,10},{1,5},{3,7},... | collective-permute-start | bytes 983048 | tf_op jit(solution)/shard_map/ppermute | solution.py:25
  34.9 6.2 %copy-start.1 = (bf16[1536,384]{1,0:T(8,128)(2,1)S(1)}, bf16[1536,384]{1,0:T(8,128)(2,1)}, u32[]{:S(2)}) copy-start(bf16[1536,384]{1,0:T(8,128)(2,1)} %w_value.1) | copy-start | bytes 3538948
  34.9 6.2 %copy-start.2 = (bf16[1536,256]{1,0:T(8,128)(2,1)S(1)}, bf16[1536,256]{1,0:T(8,128)(2,1)}, u32[]{:S(2)}) copy-start(bf16[1536,256]{1,0:T(8,128)(2,1)} %w_query.1) | copy-start | bytes 2359300
  34.9 6.2 %copy-start.3 = (bf16[1536,256]{1,0:T(8,128)(2,1)S(1)}, bf16[1536,256]{1,0:T(8,128)(2,1)}, u32[]{:S(2)}) copy-start(bf16[1536,256]{1,0:T(8,128)(2,1)} %w_key.1) | copy-start | bytes 2359300
  34.9 6.2 %copy-start.4 = (s32[16]{0:T(128)S(1)}, s32[16]{0:T(128)}, u32[]{:S(2)}) copy-start(s32[16]{0:T(128)} %positions.3) | copy-start | bytes 196
  34.9 6.2 %copy-start.5 = (f32[2]{0:T(128)S(1)}, f32[2]{0:T(128)}, u32[]{:S(2)}) copy-start(f32[2]{0:T(128)} %slopes.3) | copy-start | bytes 28
  38.2 2.9 %collective-permute-start.10 = (f32[96,768]{1,0:T(8,128)S(1)}, f32[96,768]{1,0:T(8,128)S(1)}, u32[]{:S(2)}, u32[]{:S(2)}) collective-permute-start(f32[96,768]{1,0:T(8,128)S(1)} %get-tuple-element.51.rest_0_), channel_id=1, source_target_pairs={{0,1},{1,0},{2,3},{3,2},{4,5},{5,4},{6,7},{7,6},{8,9},{9,8},{10,11... | collective-permute-start | bytes 884744 | tf_op jit(solution)/shard_map/ppermute | solution.py:381
  38.3 2.8 %collective-permute-start.12 = (f32[80,768]{1,0:T(8,128)S(1)}, f32[80,768]{1,0:T(8,128)S(1)}, u32[]{:S(2)}, u32[]{:S(2)}) collective-permute-start(f32[80,768]{1,0:T(8,128)S(1)} %get-tuple-element.54.rest_2_), channel_id=1, source_target_pairs={{0,1},{1,0},{2,3},{3,2},{4,5},{5,4},{6,7},{7,6},{8,9},{9,8},{10,11... | collective-permute-start | bytes 737288 | tf_op jit(solution)/shard_map/ppermute | solution.py:381
  38.8 2.3 %collective-permute-start.11 = (f32[80,768]{1,0:T(8,128)S(1)}, f32[80,768]{1,0:T(8,128)S(1)}, u32[]{:S(2)}, u32[]{:S(2)}) collective-permute-start(f32[80,768]{1,0:T(8,128)S(1)} %get-tuple-element.52.rest_1_), channel_id=1, source_target_pairs={{0,1},{1,0},{2,3},{3,2},{4,5},{5,4},{6,7},{7,6},{8,9},{9,8},{10,11... | collective-permute-start | bytes 737288 | tf_op jit(solution)/shard_map/ppermute | solution.py:381
  38.9 6.5 %collective-permute-start.14 = (bf16[128,640]{1,0:T(8,128)(2,1)S(1)}, bf16[128,640]{1,0:T(8,128)(2,1)S(1)}, u32[]{:S(2)}, u32[]{:S(2)}) collective-permute-start(bf16[128,640]{1,0:T(8,128)(2,1)S(1)} %collective-permute-done.8.rest_10_), channel_id=1, source_target_pairs={{0,2},{2,0},{4,6},{6,4},{8,10},{10,8},{12,14},{14,12},{1,3},{3,1},... | collective-permute-start | bytes 491528 | tf_op jit(solution)/shard_map/ppermute | solution.py:25

commit v3 on v2

--- a/solution.py
+++ b/solution.py
@@ -99,9 +99,14 @@
     taps,
     *rest,
 ):
-    *rest, held, taps32, deltas32 = rest
+    *rest, held, taps32, deltas32, spots = rest
     pieces, outs = rest[:-PARTS], rest[-PARTS:]
     channels = taps32.shape[2]
+    for v in range(block_lists.shape[1]):
+        for k in range(4):
+            slot = block_slot[block_lists[k, v]]
+            owner = lax.div(slot, per_owner)
+            spots[4 * v + k] = place_of(owner) * per_owner + lax.rem(slot, per_owner)
     taps32[...] = jnp.broadcast_to(taps[...].astype(jnp.float32)[:, None, :], taps32.shape)
     deltas32[...] = deltas[...].astype(jnp.float32)
     first = 0
@@ -117,11 +122,7 @@
     row = lax.broadcasted_iota(jnp.int32, (8, chunk), 0)
 
     def variant(out, begin, v):
-        places = []
-        for k in range(4):
-            slot = block_slot[block_lists[k, begin + v]]
-            owner = slot // per_owner
-            places.append(place_of(owner) * per_owner + slot - owner * per_owner)
+        places = [spots[4 * (begin + v) + k] for k in range(4)]
         offset = window_offsets[begin + v]
         for at in range(0, channels, chunk):
             lanes = slice(at, at + chunk)
@@ -130,14 +131,13 @@
             cells[1] = cells[1] + jnp.where(row == offset, delta, 0.0)
             cells[2] = cells[2] + jnp.where(row == offset - 8, delta, 0.0)
             early, late = jnp.stack(cells[:3]), jnp.stack(cells[1:])
-            total = None
-            for s in range(7, 0, -1):
-                term = early * taps32[s, :, lanes] + late * taps32[s + 8, :, lanes]
-                total = term if total is None else total + term
-                total = pltpu.roll(total.reshape(24, chunk), 23, 0).reshape(3, 8, chunk)
-            total = total[0:2] + early[0:2] * taps32[0, :, lanes]
+            total = early[0:2] * taps32[0, :, lanes]
             total = total + late[0:2] * (1.0 + taps32[8, :, lanes])
             total = total + late[1:3] * taps32[16, :, lanes]
+            for s in range(1, 8):
+                term = early * taps32[s, :, lanes] + late * taps32[s + 8, :, lanes]
+                term = pltpu.roll(term.reshape(24, chunk), 24 - s, 0)
+                total = total + term[:W].reshape(2, 8, chunk)
             out[pl.ds(pl.multiple_of(v * W, W), W), lanes] = total.reshape(W, chunk)
 
     begin = 0
@@ -257,6 +257,10 @@
         sums[h] = summed
 
 
+def spread(tile, width):
+    return jnp.concatenate([tile] * (width // tile.shape[1]), axis=1)
+
+
 def far_kernel(sizes, positions, slopes, queries, stats, sums, *rest):
     value_width, window_rows = sizes
     *pieces, out = rest
@@ -279,13 +283,18 @@
             firsts,
         )
         values = [piece[:, base + low : base + high] for piece in pieces]
-        before = stats[2 * h][:, :1]
+        before = stats[2 * h]
         peak = jnp.maximum(before, peak_of(scores))
-        total, summed = weigh(scores, values, peak)
         factor = jnp.exp(before - peak)
-        total = total + stats[2 * h + 1][:, :1] * factor
-        summed = summed + sums[h] * factor
-        results.append((low, high, summed * (1.0 / total)))
+        total = stats[2 * h + 1] * factor
+        summed = sums[h] * spread(factor, high - low)
+        for score, value in zip(scores, values):
+            weight = jnp.exp(score - spread(peak, score.shape[1]))
+            total = total + jnp.sum(weight, axis=1, keepdims=True)
+            summed = summed + jnp.dot(
+                weight.astype(jnp.bfloat16), value, preferred_element_type=jnp.float32
+            )
+        results.append((low, high, summed * spread(1.0 / total, high - low)))
     lane = lax.broadcasted_iota(jnp.int32, (rows, 128), 1)
     for column in range(0, heads * value_width, 128):
         merged = None
@@ -317,7 +326,7 @@
     head_slopes,
 ):
     per_owner, block_rows, channels = cache_vals.shape
-    variants = block_lists.shape[0]
+    variants, per_variant = block_lists.shape
     half = channels // lax.axis_size("rep")
     smem = pl.BlockSpec(memory_space=pltpu.SMEM)
     vmem = pl.BlockSpec(memory_space=pltpu.VMEM)
@@ -358,6 +367,7 @@
             pltpu.VMEM((held, block_rows, half), jnp.float32),
             pltpu.VMEM((TAPS, 8, half), jnp.float32),
             pltpu.VMEM((variants, half), jnp.float32),
+            pltpu.SMEM((variants * per_variant,), jnp.int32),
         ],
         compiler_params=pltpu.CompilerParams(vmem_limit_bytes=tower_limit),
         cost_estimate=pl.CostEstimate(

time: 47.4 us -> 47 us (level)
  transfers between devices with their start and end apart: 15 -> 15, of which waited for: 8 -> 8; matrix products, arithmetic and copies ran while one was open for 2% -> 2% of each run, Pallas kernels for 13% -> 12%
where the time goes in v3:
time: 47 us; the launch traced here: 46.9 us
  starting transfers between devices  21.3 us (45%)
  waiting for transfers between devices  15.8 us (34%)
  Pallas kernels  7.48 us (16%)
  local copies, waits for them, and re-layouts  1.07 us (2%)
  other arithmetic  1.03 us (2%)
    ppermute x12, starting transfers between devices, send(): return lax.ppermute(x, ('seq', 'var'), pairs)  20.6 us
    ppermute x12, waiting for transfers between devices, send(): return lax.ppermute(x, ('seq', 'var'), pairs)  15.8 us
    pallas_call x1, Pallas kernels, on_device(): pl.pallas_call(functools.partial(tower_kernel, per_owner), out_shape=towe...  2.95 us
    pallas_call x1, Pallas kernels, on_device(): pl.pallas_call(functools.partial(near_kernel, sizes), out_shape=[jax.Shap...  2.76 us
    pallas_call x1, Pallas kernels, on_device(): pl.pallas_call(functools.partial(far_kernel, sizes), out_shape=jax.ShapeD...  1.76 us
    concatenate x1, other arithmetic, on_device(): window = jnp.concatenate([ref_keys, ref_values], axis=1)  1.03 us
  transfers between devices with their start and end apart: 15, of which 8 were waited for; matrix products, arithmetic and copies ran while one was open for 2% of the time, Pallas kernels for 12%

profile of v3, /device:TPU:0, one launch (start us, length us, event | category | flops | bytes accessed | tf_op | source)
XLA Modules:
  0.0 46.9 jit_solution(17466349405361556933)
XLA Ops:
  0.0 0.0 copy-start
  0.0 0.0 copy-start.10
  0.0 0.0 copy-start.11
  0.0 0.0 copy-start.9
  0.0 0.0 copy-start.6
  0.0 0.0 copy-start.7
  0.0 0.0 copy-start.8
  0.0 0.8 %constant_dynamic-slice_fusion.4.scales = bf16[16,768]{1,0:T(8,128)(2,1)S(1)} fusion(bf16[16,1536]{1,0:T(8,128)(2,1)} %param.16, s32[]{:T(128)S(6)} %select_n.4), kind=kLoop, calls=%fused_computation.5 | loop fusion | bytes 49156 | tf_op jit(solution)/shard_map/dynamic_slice | solution.py:335
  0.8 0.2 copy-done
  1.1 3.1 %collective-permute-start.1 = (bf16[18,8,768]{2,1,0:T(8,128)(2,1)S(1)}, bf16[18,8,768]{2,1,0:T(8,128)(2,1)S(1)}, u32[]{:S(2)}, u32[]{:S(2)}) collective-permute-start(bf16[18,8,768]{2,1,0:T(8,128)(2,1)S(1)} %pack.1), channel_id=1, source_target_pairs={{0,4},{2,6},{4,0},{6,2},{8,12},{10,14},{12,8},{14,10},{1,5},{3,7},... | collective-permute-start | bytes 663560 | tf_op jit(solution)/shard_map/ppermute | solution.py:25
  4.1 1.5 %collective-permute-start.2 = (bf16[18,8,768]{2,1,0:T(8,128)(2,1)S(1)}, bf16[18,8,768]{2,1,0:T(8,128)(2,1)S(1)}, u32[]{:S(2)}, u32[]{:S(2)}) collective-permute-start(bf16[18,8,768]{2,1,0:T(8,128)(2,1)S(1)} %pack.1), channel_id=1, source_target_pairs={{0,2},{2,0},{4,6},{6,4},{8,10},{10,8},{12,14},{14,12},{1,3},{3,1},... | collective-permute-start | bytes 663560 | tf_op jit(solution)/shard_map/ppermute | solution.py:25
  5.6 2.5 %collective-permute-start = (bf16[18,8,768]{2,1,0:T(8,128)(2,1)S(1)}, bf16[18,8,768]{2,1,0:T(8,128)(2,1)S(1)}, u32[]{:S(2)}, u32[]{:S(2)}) collective-permute-start(bf16[18,8,768]{2,1,0:T(8,128)(2,1)S(1)} %pack.1), channel_id=1, source_target_pairs={{0,12},{2,14},{4,8},{6,10},{8,4},{10,6},{12,0},{14,2},{1,13},{3,15... | collective-permute-start | bytes 663560 | tf_op jit(solution)/shard_map/ppermute | solution.py:25
  8.1 1.0 %pad_maximum_fusion.rest_6_ = bf16[256,640]{1,0:T(8,128)(2,1)S(1)} fusion(bf16[256,384]{1,0:T(8,128)(2,1)} %param.28, bf16[256,256]{1,0:T(8,128)(2,1)} %param.27), kind=kLoop, calls=%fused_computation | loop fusion | flops 655360 | bytes 655360 | tf_op jit(solution)/shard_map/concatenate | solution.py:347
  9.1 0.8 %collective-permute-done.1 = bf16[18,8,768]{2,1,0:T(8,128)(2,1)S(1)} collective-permute-done((bf16[18,8,768]{2,1,0:T(8,128)(2,1)S(1)}, bf16[18,8,768]{2,1,0:T(8,128)(2,1)S(1)}, u32[]{:S(2)}, u32[]{:S(2)}) %collective-permute-start.1) | collective-permute-done | bytes 221216 | tf_op jit(solution)/shard_map/ppermute | solution.py:25
  10.0 1.1 %collective-permute-done.2 = bf16[18,8,768]{2,1,0:T(8,128)(2,1)S(1)} collective-permute-done((bf16[18,8,768]{2,1,0:T(8,128)(2,1)S(1)}, bf16[18,8,768]{2,1,0:T(8,128)(2,1)S(1)}, u32[]{:S(2)}, u32[]{:S(2)}) %collective-permute-start.2) | collective-permute-done | bytes 221216 | tf_op jit(solution)/shard_map/ppermute | solution.py:25
  11.0 1.5 %collective-permute-start.3 = (bf16[18,8,768]{2,1,0:T(8,128)(2,1)S(1)}, bf16[18,8,768]{2,1,0:T(8,128)(2,1)S(1)}, u32[]{:S(2)}, u32[]{:S(2)}) collective-permute-start(bf16[18,8,768]{2,1,0:T(8,128)(2,1)S(1)} %collective-permute-done.1), channel_id=1, source_target_pairs={{0,2},{2,0},{4,6},{6,4},{8,10},{10,8},{12,14},{14,12},{1,3},{3,1},... | collective-permute-start | bytes 663560 | tf_op jit(solution)/shard_map/ppermute | solution.py:25
  12.5 0.0 copy-done.10
  12.5 0.0 copy-done.11
  12.5 0.0 copy-done.9
  12.6 4.0 %collective-permute-done = bf16[18,8,768]{2,1,0:T(8,128)(2,1)S(1)} collective-permute-done((bf16[18,8,768]{2,1,0:T(8,128)(2,1)S(1)}, bf16[18,8,768]{2,1,0:T(8,128)(2,1)S(1)}, u32[]{:S(2)}, u32[]{:S(2)}) %collective-permute-start) | collective-permute-done | bytes 221216 | tf_op jit(solution)/shard_map/ppermute | solution.py:25
  16.6 1.8 %collective-permute-start.4 = (bf16[18,8,768]{2,1,0:T(8,128)(2,1)S(1)}, bf16[18,8,768]{2,1,0:T(8,128)(2,1)S(1)}, u32[]{:S(2)}, u32[]{:S(2)}) collective-permute-start(bf16[18,8,768]{2,1,0:T(8,128)(2,1)S(1)} %collective-permute-done), channel_id=1, source_target_pairs={{0,4},{2,6},{4,0},{6,2},{8,12},{10,14},{12,8},{14,10},{1,5},{3,7},... | collective-permute-start | bytes 663560 | tf_op jit(solution)/shard_map/ppermute | solution.py:25
  18.4 0.0 collective-permute-done.3
  18.4 0.5 %collective-permute-start.6 = (bf16[18,8,768]{2,1,0:T(8,128)(2,1)S(1)}, bf16[18,8,768]{2,1,0:T(8,128)(2,1)S(1)}, u32[]{:S(2)}, u32[]{:S(2)}) collective-permute-start(bf16[18,8,768]{2,1,0:T(8,128)(2,1)S(1)} %collective-permute-done), channel_id=1, source_target_pairs={{0,2},{2,0},{4,6},{6,4},{8,10},{10,8},{12,14},{14,12},{1,3},{3,1},... | collective-permute-start | bytes 663560 | tf_op jit(solution)/shard_map/ppermute | solution.py:25
  19.0 3.9 %collective-permute-done.4 = bf16[18,8,768]{2,1,0:T(8,128)(2,1)S(1)} collective-permute-done((bf16[18,8,768]{2,1,0:T(8,128)(2,1)S(1)}, bf16[18,8,768]{2,1,0:T(8,128)(2,1)S(1)}, u32[]{:S(2)}, u32[]{:S(2)}) %collective-permute-start.4) | collective-permute-done | bytes 221216 | tf_op jit(solution)/shard_map/ppermute | solution.py:25
  22.8 4.3 %collective-permute-start.7 = (bf16[128,640]{1,0:T(8,128)(2,1)S(1)}, bf16[128,640]{1,0:T(8,128)(2,1)S(1)}, u32[]{:S(2)}, u32[]{:S(2)}) collective-permute-start(bf16[128,640]{1,0:T(8,128)(2,1)S(1)} %constant_dynamic-slice_fusion), channel_id=1, source_target_pairs={{0,12},{2,14},{4,8},{6,10},{8,4},{10,6},{12,0},{14,2},{1,13},{3,15... | collective-permute-start | bytes 491528 | tf_op jit(solution)/shard_map/ppermute | solution.py:25
  27.2 1.0 %collective-permute-start.5 = (bf16[18,8,768]{2,1,0:T(8,128)(2,1)S(1)}, bf16[18,8,768]{2,1,0:T(8,128)(2,1)S(1)}, u32[]{:S(2)}, u32[]{:S(2)}) collective-permute-start(bf16[18,8,768]{2,1,0:T(8,128)(2,1)S(1)} %collective-permute-done.4), channel_id=1, source_target_pairs={{0,2},{2,0},{4,6},{6,4},{8,10},{10,8},{12,14},{14,12},{1,3},{3,1},... | collective-permute-start | bytes 663560 | tf_op jit(solution)/shard_map/ppermute | solution.py:25
  28.2 3.0 %collective-permute-done.7.rest_8_ = bf16[128,640]{1,0:T(8,128)(2,1)S(1)} collective-permute-done((bf16[128,640]{1,0:T(8,128)(2,1)S(1)}, bf16[128,640]{1,0:T(8,128)(2,1)S(1)}, u32[]{:S(2)}, u32[]{:S(2)}) %collective-permute-start.7) | collective-permute-done | bytes 163872 | tf_op jit(solution)/shard_map/ppermute | solution.py:25
  31.1 0.0 collective-permute-done.6
  31.2 0.7 %collective-permute-start.8 = (bf16[128,640]{1,0:T(8,128)(2,1)S(1)}, bf16[128,640]{1,0:T(8,128)(2,1)S(1)}, u32[]{:S(2)}, u32[]{:S(2)}) collective-permute-start(bf16[128,640]{1,0:T(8,128)(2,1)S(1)} %collective-permute-done.7.rest_8_), channel_id=1, source_target_pairs={{0,4},{2,6},{4,0},{6,2},{8,12},{10,14},{12,8},{14,10},{1,5},{3,7},... | collective-permute-start | bytes 491528 | tf_op jit(solution)/shard_map/ppermute | solution.py:25
  31.8 0.9 %collective-permute-start.9 = (bf16[128,640]{1,0:T(8,128)(2,1)S(1)}, bf16[128,640]{1,0:T(8,128)(2,1)S(1)}, u32[]{:S(2)}, u32[]{:S(2)}) collective-permute-start(bf16[128,640]{1,0:T(8,128)(2,1)S(1)} %collective-permute-done.7.rest_8_), channel_id=1, source_target_pairs={{0,2},{2,0},{4,6},{6,4},{8,10},{10,8},{12,14},{14,12},{1,3},{3,1},... | collective-permute-start | bytes 491528 | tf_op jit(solution)/shard_map/ppermute | solution.py:25
  32.7 2.0 %collective-permute-start.13 = (bf16[256,640]{1,0:T(8,128)(2,1)S(1)}, bf16[256,640]{1,0:T(8,128)(2,1)S(1)}, u32[]{:S(2)}, u32[]{:S(2)}) collective-permute-start(bf16[256,640]{1,0:T(8,128)(2,1)S(1)} %pad_maximum_fusion.rest_6_), channel_id=1, source_target_pairs={{0,4},{2,6},{4,0},{6,2},{8,12},{10,14},{12,8},{14,10},{1,5},{3,7},... | collective-permute-start | bytes 983048 | tf_op jit(solution)/shard_map/ppermute | solution.py:25
  34.8 0.1 collective-permute-done.5
  34.9 0.0 copy-done.6
  34.9 0.0 copy-done.7
  34.9 0.0 copy-done.8
  34.9 0.0 copy-start.1
  34.9 0.0 copy-start.2
  34.9 0.0 copy-start.3
  34.9 0.0 copy-start.4
  34.9 0.0 copy-start.5
  34.9 2.9 %tower.1 = (f32[96,768]{1,0:T(8,128)S(1)}, f32[80,768]{1,0:T(8,128)S(1)}, f32[80,768]{1,0:T(8,128)S(1)}) custom-call(s32[128]{0:T(128)S(1)} %copy-done.7, s32[4,16]{1,0:T(4,128)S(1)} %bitcast.18, s32[16]{0:T(128)S(1)} %copy-done.8, bf16[16,768]{1,0:T(8,128)(2,1)S(1)} %constant_dynamic-slice_fusion.2.deltas, ...), custom_call_target="tpu_custom_call" | custom-call | flops 1000000000 | bytes 40000000 | tf_op jit(solution)/shard_map/tower/pallas_call | solution.py:361
  37.9 0.0 collective-permute-done.8.rest_10_
  37.9 0.1 collective-permute-start.10
  38.0 0.0 collective-permute-done.9.rest_9_
  38.0 0.5 %collective-permute-start.12 = (f32[80,768]{1,0:T(8,128)S(1)}, f32[80,768]{1,0:T(8,128)S(1)}, u32[]{:S(2)}, u32[]{:S(2)}) collective-permute-start(f32[80,768]{1,0:T(8,128)S(1)} %get-tuple-element.54.rest_2_), channel_id=1, source_target_pairs={{0,1},{1,0},{2,3},{3,2},{4,5},{5,4},{6,7},{7,6},{8,9},{9,8},{10,11... | collective-permute-start | bytes 737288 | tf_op jit(solution)/shard_map/ppermute | solution.py:391
  38.5 0.1 collective-permute-start.11
  38.6 0.8 %collective-permute-start.14 = (bf16[128,640]{1,0:T(8,128)(2,1)S(1)}, bf16[128,640]{1,0:T(8,128)(2,1)S(1)}, u32[]{:S(2)}, u32[]{:S(2)}) collective-permute-start(bf16[128,640]{1,0:T(8,128)(2,1)S(1)} %collective-permute-done.8.rest_10_), channel_id=1, source_target_pairs={{0,2},{2,0},{4,6},{6,4},{8,10},{10,8},{12,14},{14,12},{1,3},{3,1},... | collective-permute-start | bytes 491528 | tf_op jit(solution)/shard_map/ppermute | solution.py:25
  39.4 1.7 %collective-permute-done.13.rest_7_ = bf16[256,640]{1,0:T(8,128)(2,1)S(1)} collective-permute-done((bf16[256,640]{1,0:T(8,128)(2,1)S(1)}, bf16[256,640]{1,0:T(8,128)(2,1)S(1)}, u32[]{:S(2)}, u32[]{:S(2)}) %collective-permute-start.13) | collective-permute-done | bytes 327712 | tf_op jit(solution)/shard_map/ppermute | solution.py:25
  41.1 0.0 collective-permute-done.12.rest_5_
  41.1 0.0 collective-permute-done.11.rest_4_
  41.1 0.0 collective-permute-done.10.rest_3_
  41.1 0.0 copy-done.1
  41.1 0.0 copy-done.2
  41.1 0.0 copy-done.3
  41.2 0.0 copy-done.4
  41.2 0.0 copy-done.5
  41.2 2.8 %near.1 = (bf16[256,256]{1,0:T(8,128)(2,1)S(1)}, f32[4,256,128]{2,1,0:T(8,128)S(1)}, f32[2,256,256]{2,1,0:T(8,128)S(1)}) custom-call(s32[16]{0:T(128)S(1)} %copy-done.4, f32[2]{0:T(128)S(1)} %copy-done.5, f32[1,1536]{1,0:T(1,128)S(1)} %reshape.6.gain, bf16[1536,256]{1,0:T(8,128)(2,1)S(1)} %copy-done.2, bf16[1536,256]{1,0:T(8,128)(2,1)S(1)} %copy-done.3, ...), custom_call_target="tpu_custom_call" | custom-call | tf_op jit(solution)/shard_map/near/pallas_call | solution.py:397
  43.9 1.2 %collective-permute-done.14.rest_0_ = bf16[128,640]{1,0:T(8,128)(2,1)S(1)} collective-permute-done((bf16[128,640]{1,0:T(8,128)(2,1)S(1)}, bf16[128,640]{1,0:T(8,128)(2,1)S(1)}, u32[]{:S(2)}, u32[]{:S(2)}) %collective-permute-start.14) | collective-permute-done | bytes 163872 | tf_op jit(solution)/shard_map/ppermute | solution.py:25
  45.1 1.8 %far.1 = bf16[256,384]{1,0:T(8,128)(2,1)} custom-call(s32[16]{0:T(128)S(1)} %copy-done.4, f32[2]{0:T(128)S(1)} %copy-done.5, bf16[256,256]{1,0:T(8,128)(2,1)S(1)} %get-tuple-element.58.queries, f32[4,256,128]{2,1,0:T(8,128)S(1)} %get-tuple-element.59.stats, f32[2,256,256]{2,1,0:T(8,128)S(1)} %get-tuple-element.60.sums, ...), custom_call_target="tpu_custom_call" | custom-call | tf_op jit(solution)/shard_map/far/pallas_call | solution.py:419
  (6 shorter events, 0.1 us)
Async XLA Ops:
  0.0 1.0 %copy-start = (bf16[16,8,1536]{2,1,0:T(8,128)(2,1)S(1)}, bf16[16,8,1536]{2,1,0:T(8,128)(2,1)}, u32[]{:S(2)}) copy-start(bf16[16,8,1536]{2,1,0:T(8,128)(2,1)} %param.15) | copy-start | bytes 1179652
  0.0 12.5 %copy-start.10 = (bf16[16,1536]{1,0:T(8,128)(2,1)S(1)}, bf16[16,1536]{1,0:T(8,128)(2,1)}, u32[]{:S(2)}) copy-start(bf16[16,1536]{1,0:T(8,128)(2,1)} %param.21) | copy-start | bytes 147460
  0.0 12.5 %copy-start.11 = (f32[1536]{0:T(1024)S(1)}, f32[1536]{0:T(1024)}, u32[]{:S(2)}) copy-start(f32[1536]{0:T(1024)} %param.23) | copy-start | bytes 18436
  0.0 12.5 %copy-start.9 = (bf16[17,1536]{1,0:T(8,128)(2,1)S(1)}, bf16[17,1536]{1,0:T(8,128)(2,1)}, u32[]{:S(2)}) copy-start(bf16[17,1536]{1,0:T(8,128)(2,1)} %param.22) | copy-start | bytes 156676
  0.0 34.9 %copy-start.6 = (s32[16,4]{0,1:T(4,128)S(1)}, s32[16,4]{0,1:T(4,128)}, u32[]{:S(2)}) copy-start(s32[16,4]{0,1:T(4,128)} %param.18) | copy-start | bytes 772
  0.0 34.9 %copy-start.7 = (s32[128]{0:T(128)S(1)}, s32[128]{0:T(128)}, u32[]{:S(2)}) copy-start(s32[128]{0:T(128)} %block_slot.1) | copy-start | bytes 1540
  0.0 34.8 %copy-start.8 = (s32[16]{0:T(128)S(1)}, s32[16]{0:T(128)}, u32[]{:S(2)}) copy-start(s32[16]{0:T(128)} %window_offsets.1) | copy-start | bytes 196
  1.1 8.9 %collective-permute-start.1 = (bf16[18,8,768]{2,1,0:T(8,128)(2,1)S(1)}, bf16[18,8,768]{2,1,0:T(8,128)(2,1)S(1)}, u32[]{:S(2)}, u32[]{:S(2)}) collective-permute-start(bf16[18,8,768]{2,1,0:T(8,128)(2,1)S(1)} %pack.1), channel_id=1, source_target_pairs={{0,4},{2,6},{4,0},{6,2},{8,12},{10,14},{12,8},{14,10},{1,5},{3,7},... | collective-permute-start | bytes 663560 | tf_op jit(solution)/shard_map/ppermute | solution.py:25
  4.1 6.9 %collective-permute-start.2 = (bf16[18,8,768]{2,1,0:T(8,128)(2,1)S(1)}, bf16[18,8,768]{2,1,0:T(8,128)(2,1)S(1)}, u32[]{:S(2)}, u32[]{:S(2)}) collective-permute-start(bf16[18,8,768]{2,1,0:T(8,128)(2,1)S(1)} %pack.1), channel_id=1, source_target_pairs={{0,2},{2,0},{4,6},{6,4},{8,10},{10,8},{12,14},{14,12},{1,3},{3,1},... | collective-permute-start | bytes 663560 | tf_op jit(solution)/shard_map/ppermute | solution.py:25
  5.6 11.0 %collective-permute-start = (bf16[18,8,768]{2,1,0:T(8,128)(2,1)S(1)}, bf16[18,8,768]{2,1,0:T(8,128)(2,1)S(1)}, u32[]{:S(2)}, u32[]{:S(2)}) collective-permute-start(bf16[18,8,768]{2,1,0:T(8,128)(2,1)S(1)} %pack.1), channel_id=1, source_target_pairs={{0,12},{2,14},{4,8},{6,10},{8,4},{10,6},{12,0},{14,2},{1,13},{3,15... | collective-permute-start | bytes 663560 | tf_op jit(solution)/shard_map/ppermute | solution.py:25
  11.0 7.4 %collective-permute-start.3 = (bf16[18,8,768]{2,1,0:T(8,128)(2,1)S(1)}, bf16[18,8,768]{2,1,0:T(8,128)(2,1)S(1)}, u32[]{:S(2)}, u32[]{:S(2)}) collective-permute-start(bf16[18,8,768]{2,1,0:T(8,128)(2,1)S(1)} %collective-permute-done.1), channel_id=1, source_target_pairs={{0,2},{2,0},{4,6},{6,4},{8,10},{10,8},{12,14},{14,12},{1,3},{3,1},... | collective-permute-start | bytes 663560 | tf_op jit(solution)/shard_map/ppermute | solution.py:25
  16.6 6.2 %collective-permute-start.4 = (bf16[18,8,768]{2,1,0:T(8,128)(2,1)S(1)}, bf16[18,8,768]{2,1,0:T(8,128)(2,1)S(1)}, u32[]{:S(2)}, u32[]{:S(2)}) collective-permute-start(bf16[18,8,768]{2,1,0:T(8,128)(2,1)S(1)} %collective-permute-done), channel_id=1, source_target_pairs={{0,4},{2,6},{4,0},{6,2},{8,12},{10,14},{12,8},{14,10},{1,5},{3,7},... | collective-permute-start | bytes 663560 | tf_op jit(solution)/shard_map/ppermute | solution.py:25
  18.4 12.8 %collective-permute-start.6 = (bf16[18,8,768]{2,1,0:T(8,128)(2,1)S(1)}, bf16[18,8,768]{2,1,0:T(8,128)(2,1)S(1)}, u32[]{:S(2)}, u32[]{:S(2)}) collective-permute-start(bf16[18,8,768]{2,1,0:T(8,128)(2,1)S(1)} %collective-permute-done), channel_id=1, source_target_pairs={{0,2},{2,0},{4,6},{6,4},{8,10},{10,8},{12,14},{14,12},{1,3},{3,1},... | collective-permute-start | bytes 663560 | tf_op jit(solution)/shard_map/ppermute | solution.py:25
  22.8 8.3 %collective-permute-start.7 = (bf16[128,640]{1,0:T(8,128)(2,1)S(1)}, bf16[128,640]{1,0:T(8,128)(2,1)S(1)}, u32[]{:S(2)}, u32[]{:S(2)}) collective-permute-start(bf16[128,640]{1,0:T(8,128)(2,1)S(1)} %constant_dynamic-slice_fusion), channel_id=1, source_target_pairs={{0,12},{2,14},{4,8},{6,10},{8,4},{10,6},{12,0},{14,2},{1,13},{3,15... | collective-permute-start | bytes 491528 | tf_op jit(solution)/shard_map/ppermute | solution.py:25
  27.2 7.7 %collective-permute-start.5 = (bf16[18,8,768]{2,1,0:T(8,128)(2,1)S(1)}, bf16[18,8,768]{2,1,0:T(8,128)(2,1)S(1)}, u32[]{:S(2)}, u32[]{:S(2)}) collective-permute-start(bf16[18,8,768]{2,1,0:T(8,128)(2,1)S(1)} %collective-permute-done.4), channel_id=1, source_target_pairs={{0,2},{2,0},{4,6},{6,4},{8,10},{10,8},{12,14},{14,12},{1,3},{3,1},... | collective-permute-start | bytes 663560 | tf_op jit(solution)/shard_map/ppermute | solution.py:25
  31.2 6.7 %collective-permute-start.8 = (bf16[128,640]{1,0:T(8,128)(2,1)S(1)}, bf16[128,640]{1,0:T(8,128)(2,1)S(1)}, u32[]{:S(2)}, u32[]{:S(2)}) collective-permute-start(bf16[128,640]{1,0:T(8,128)(2,1)S(1)} %collective-permute-done.7.rest_8_), channel_id=1, source_target_pairs={{0,4},{2,6},{4,0},{6,2},{8,12},{10,14},{12,8},{14,10},{1,5},{3,7},... | collective-permute-start | bytes 491528 | tf_op jit(solution)/shard_map/ppermute | solution.py:25
  31.8 6.1 %collective-permute-start.9 = (bf16[128,640]{1,0:T(8,128)(2,1)S(1)}, bf16[128,640]{1,0:T(8,128)(2,1)S(1)}, u32[]{:S(2)}, u32[]{:S(2)}) collective-permute-start(bf16[128,640]{1,0:T(8,128)(2,1)S(1)} %collective-permute-done.7.rest_8_), channel_id=1, source_target_pairs={{0,2},{2,0},{4,6},{6,4},{8,10},{10,8},{12,14},{14,12},{1,3},{3,1},... | collective-permute-start | bytes 491528 | tf_op jit(solution)/shard_map/ppermute | solution.py:25
  32.7 8.4 %collective-permute-start.13 = (bf16[256,640]{1,0:T(8,128)(2,1)S(1)}, bf16[256,640]{1,0:T(8,128)(2,1)S(1)}, u32[]{:S(2)}, u32[]{:S(2)}) collective-permute-start(bf16[256,640]{1,0:T(8,128)(2,1)S(1)} %pad_maximum_fusion.rest_6_), channel_id=1, source_target_pairs={{0,4},{2,6},{4,0},{6,2},{8,12},{10,14},{12,8},{14,10},{1,5},{3,7},... | collective-permute-start | bytes 983048 | tf_op jit(solution)/shard_map/ppermute | solution.py:25
  34.9 6.2 %copy-start.1 = (bf16[1536,384]{1,0:T(8,128)(2,1)S(1)}, bf16[1536,384]{1,0:T(8,128)(2,1)}, u32[]{:S(2)}) copy-start(bf16[1536,384]{1,0:T(8,128)(2,1)} %w_value.1) | copy-start | bytes 3538948
  34.9 6.2 %copy-start.2 = (bf16[1536,256]{1,0:T(8,128)(2,1)S(1)}, bf16[1536,256]{1,0:T(8,128)(2,1)}, u32[]{:S(2)}) copy-start(bf16[1536,256]{1,0:T(8,128)(2,1)} %w_query.1) | copy-start | bytes 2359300
  34.9 6.2 %copy-start.3 = (bf16[1536,256]{1,0:T(8,128)(2,1)S(1)}, bf16[1536,256]{1,0:T(8,128)(2,1)}, u32[]{:S(2)}) copy-start(bf16[1536,256]{1,0:T(8,128)(2,1)} %w_key.1) | copy-start | bytes 2359300
  34.9 6.2 %copy-start.4 = (s32[16]{0:T(128)S(1)}, s32[16]{0:T(128)}, u32[]{:S(2)}) copy-start(s32[16]{0:T(128)} %positions.3) | copy-start | bytes 196
  34.9 6.2 %copy-start.5 = (f32[2]{0:T(128)S(1)}, f32[2]{0:T(128)}, u32[]{:S(2)}) copy-start(f32[2]{0:T(128)} %slopes.3) | copy-start | bytes 28
  37.9 3.2 %collective-permute-start.10 = (f32[96,768]{1,0:T(8,128)S(1)}, f32[96,768]{1,0:T(8,128)S(1)}, u32[]{:S(2)}, u32[]{:S(2)}) collective-permute-start(f32[96,768]{1,0:T(8,128)S(1)} %get-tuple-element.51.rest_0_), channel_id=1, source_target_pairs={{0,1},{1,0},{2,3},{3,2},{4,5},{5,4},{6,7},{7,6},{8,9},{9,8},{10,11... | collective-permute-start | bytes 884744 | tf_op jit(solution)/shard_map/ppermute | solution.py:391
  38.0 3.1 %collective-permute-start.12 = (f32[80,768]{1,0:T(8,128)S(1)}, f32[80,768]{1,0:T(8,128)S(1)}, u32[]{:S(2)}, u32[]{:S(2)}) collective-permute-start(f32[80,768]{1,0:T(8,128)S(1)} %get-tuple-element.54.rest_2_), channel_id=1, source_target_pairs={{0,1},{1,0},{2,3},{3,2},{4,5},{5,4},{6,7},{7,6},{8,9},{9,8},{10,11... | collective-permute-start | bytes 737288 | tf_op jit(solution)/shard_map/ppermute | solution.py:391
  38.5 2.6 %collective-permute-start.11 = (f32[80,768]{1,0:T(8,128)S(1)}, f32[80,768]{1,0:T(8,128)S(1)}, u32[]{:S(2)}, u32[]{:S(2)}) collective-permute-start(f32[80,768]{1,0:T(8,128)S(1)} %get-tuple-element.52.rest_1_), channel_id=1, source_target_pairs={{0,1},{1,0},{2,3},{3,2},{4,5},{5,4},{6,7},{7,6},{8,9},{9,8},{10,11... | collective-permute-start | bytes 737288 | tf_op jit(solution)/shard_map/ppermute | solution.py:391
  38.6 6.5 %collective-permute-start.14 = (bf16[128,640]{1,0:T(8,128)(2,1)S(1)}, bf16[128,640]{1,0:T(8,128)(2,1)S(1)}, u32[]{:S(2)}, u32[]{:S(2)}) collective-permute-start(bf16[128,640]{1,0:T(8,128)(2,1)S(1)} %collective-permute-done.8.rest_10_), channel_id=1, source_target_pairs={{0,2},{2,0},{4,6},{6,4},{8,10},{10,8},{12,14},{14,12},{1,3},{3,1},... | collective-permute-start | bytes 491528 | tf_op jit(solution)/shard_map/ppermute | solution.py:25

commit v4 on v3

--- a/solution.py
+++ b/solution.py
@@ -142,7 +142,7 @@
 
     begin = 0
     for out in outs:
-        pl.loop(0, out.shape[0] // W)(functools.partial(variant, out, begin))
+        pl.loop(0, out.shape[0] // W, unroll=True)(functools.partial(variant, out, begin))
         begin += out.shape[0] // W
 
 

time: 47 us -> 46.6 us (level)
  transfers between devices with their start and end apart: 15 -> 15, of which waited for: 8 -> 9; matrix products, arithmetic and copies ran while one was open for 2% -> 2% of each run, Pallas kernels for 12% -> 11%
where the time goes in v4:
time: 46.6 us; the launch traced here: 46.5 us
  starting transfers between devices  21.6 us (46%)
  waiting for transfers between devices  15.5 us (33%)
  Pallas kernels  7.1 us (15%)
  local copies, waits for them, and re-layouts  1.07 us (2%)
  other arithmetic  1.03 us (2%)
    ppermute x12, starting transfers between devices, send(): return lax.ppermute(x, ('seq', 'var'), pairs)  21 us
    ppermute x12, waiting for transfers between devices, send(): return lax.ppermute(x, ('seq', 'var'), pairs)  15.5 us
    pallas_call x1, Pallas kernels, on_device(): pl.pallas_call(functools.partial(near_kernel, sizes), out_shape=[jax.Shap...  2.76 us
    pallas_call x1, Pallas kernels, on_device(): pl.pallas_call(functools.partial(tower_kernel, per_owner), out_shape=towe...  2.57 us
    pallas_call x1, Pallas kernels, on_device(): pl.pallas_call(functools.partial(far_kernel, sizes), out_shape=jax.ShapeD...  1.76 us
    concatenate x1, other arithmetic, on_device(): window = jnp.concatenate([ref_keys, ref_values], axis=1)  1.03 us
  transfers between devices with their start and end apart: 15, of which 9 were waited for; matrix products, arithmetic and copies ran while one was open for 2% of the time, Pallas kernels for 11%

profile of v4, /device:TPU:0, one launch (start us, length us, event | category | flops | bytes accessed | tf_op | source)
XLA Modules:
  0.0 46.5 jit_solution(8192125504762581756)
XLA Ops:
  0.0 0.0 copy-start
  0.0 0.0 copy-start.10
  0.0 0.0 copy-start.11
  0.0 0.0 copy-start.9
  0.0 0.0 copy-start.6
  0.0 0.0 copy-start.7
  0.0 0.0 copy-start.8
  0.0 0.8 %constant_dynamic-slice_fusion.4.scales = bf16[16,768]{1,0:T(8,128)(2,1)S(1)} fusion(bf16[16,1536]{1,0:T(8,128)(2,1)} %param.16, s32[]{:T(128)S(6)} %select_n.4), kind=kLoop, calls=%fused_computation.5 | loop fusion | bytes 49156 | tf_op jit(solution)/shard_map/dynamic_slice | solution.py:335
  0.8 0.2 copy-done
  1.1 3.1 %collective-permute-start.1 = (bf16[18,8,768]{2,1,0:T(8,128)(2,1)S(1)}, bf16[18,8,768]{2,1,0:T(8,128)(2,1)S(1)}, u32[]{:S(2)}, u32[]{:S(2)}) collective-permute-start(bf16[18,8,768]{2,1,0:T(8,128)(2,1)S(1)} %pack.1), channel_id=1, source_target_pairs={{0,4},{2,6},{4,0},{6,2},{8,12},{10,14},{12,8},{14,10},{1,5},{3,7},... | collective-permute-start | bytes 663560 | tf_op jit(solution)/shard_map/ppermute | solution.py:25
  4.1 1.5 %collective-permute-start.2 = (bf16[18,8,768]{2,1,0:T(8,128)(2,1)S(1)}, bf16[18,8,768]{2,1,0:T(8,128)(2,1)S(1)}, u32[]{:S(2)}, u32[]{:S(2)}) collective-permute-start(bf16[18,8,768]{2,1,0:T(8,128)(2,1)S(1)} %pack.1), channel_id=1, source_target_pairs={{0,2},{2,0},{4,6},{6,4},{8,10},{10,8},{12,14},{14,12},{1,3},{3,1},... | collective-permute-start | bytes 663560 | tf_op jit(solution)/shard_map/ppermute | solution.py:25
  5.6 2.5 %collective-permute-start = (bf16[18,8,768]{2,1,0:T(8,128)(2,1)S(1)}, bf16[18,8,768]{2,1,0:T(8,128)(2,1)S(1)}, u32[]{:S(2)}, u32[]{:S(2)}) collective-permute-start(bf16[18,8,768]{2,1,0:T(8,128)(2,1)S(1)} %pack.1), channel_id=1, source_target_pairs={{0,12},{2,14},{4,8},{6,10},{8,4},{10,6},{12,0},{14,2},{1,13},{3,15... | collective-permute-start | bytes 663560 | tf_op jit(solution)/shard_map/ppermute | solution.py:25
  8.1 1.0 %pad_maximum_fusion.rest_6_ = bf16[256,640]{1,0:T(8,128)(2,1)S(1)} fusion(bf16[256,384]{1,0:T(8,128)(2,1)} %param.28, bf16[256,256]{1,0:T(8,128)(2,1)} %param.27), kind=kLoop, calls=%fused_computation | loop fusion | flops 655360 | bytes 655360 | tf_op jit(solution)/shard_map/concatenate | solution.py:347
  9.1 0.8 %collective-permute-done.1 = bf16[18,8,768]{2,1,0:T(8,128)(2,1)S(1)} collective-permute-done((bf16[18,8,768]{2,1,0:T(8,128)(2,1)S(1)}, bf16[18,8,768]{2,1,0:T(8,128)(2,1)S(1)}, u32[]{:S(2)}, u32[]{:S(2)}) %collective-permute-start.1) | collective-permute-done | bytes 221216 | tf_op jit(solution)/shard_map/ppermute | solution.py:25
  10.0 1.1 %collective-permute-done.2 = bf16[18,8,768]{2,1,0:T(8,128)(2,1)S(1)} collective-permute-done((bf16[18,8,768]{2,1,0:T(8,128)(2,1)S(1)}, bf16[18,8,768]{2,1,0:T(8,128)(2,1)S(1)}, u32[]{:S(2)}, u32[]{:S(2)}) %collective-permute-start.2) | collective-permute-done | bytes 221216 | tf_op jit(solution)/shard_map/ppermute | solution.py:25
  11.0 1.5 %collective-permute-start.3 = (bf16[18,8,768]{2,1,0:T(8,128)(2,1)S(1)}, bf16[18,8,768]{2,1,0:T(8,128)(2,1)S(1)}, u32[]{:S(2)}, u32[]{:S(2)}) collective-permute-start(bf16[18,8,768]{2,1,0:T(8,128)(2,1)S(1)} %collective-permute-done.1), channel_id=1, source_target_pairs={{0,2},{2,0},{4,6},{6,4},{8,10},{10,8},{12,14},{14,12},{1,3},{3,1},... | collective-permute-start | bytes 663560 | tf_op jit(solution)/shard_map/ppermute | solution.py:25
  12.5 0.0 copy-done.10
  12.5 0.0 copy-done.11
  12.5 0.0 copy-done.9
  12.6 4.0 %collective-permute-done = bf16[18,8,768]{2,1,0:T(8,128)(2,1)S(1)} collective-permute-done((bf16[18,8,768]{2,1,0:T(8,128)(2,1)S(1)}, bf16[18,8,768]{2,1,0:T(8,128)(2,1)S(1)}, u32[]{:S(2)}, u32[]{:S(2)}) %collective-permute-start) | collective-permute-done | bytes 221216 | tf_op jit(solution)/shard_map/ppermute | solution.py:25
  16.6 1.8 %collective-permute-start.4 = (bf16[18,8,768]{2,1,0:T(8,128)(2,1)S(1)}, bf16[18,8,768]{2,1,0:T(8,128)(2,1)S(1)}, u32[]{:S(2)}, u32[]{:S(2)}) collective-permute-start(bf16[18,8,768]{2,1,0:T(8,128)(2,1)S(1)} %collective-permute-done), channel_id=1, source_target_pairs={{0,4},{2,6},{4,0},{6,2},{8,12},{10,14},{12,8},{14,10},{1,5},{3,7},... | collective-permute-start | bytes 663560 | tf_op jit(solution)/shard_map/ppermute | solution.py:25
  18.4 0.0 collective-permute-done.3
  18.4 0.5 %collective-permute-start.6 = (bf16[18,8,768]{2,1,0:T(8,128)(2,1)S(1)}, bf16[18,8,768]{2,1,0:T(8,128)(2,1)S(1)}, u32[]{:S(2)}, u32[]{:S(2)}) collective-permute-start(bf16[18,8,768]{2,1,0:T(8,128)(2,1)S(1)} %collective-permute-done), channel_id=1, source_target_pairs={{0,2},{2,0},{4,6},{6,4},{8,10},{10,8},{12,14},{14,12},{1,3},{3,1},... | collective-permute-start | bytes 663560 | tf_op jit(solution)/shard_map/ppermute | solution.py:25
  19.0 3.9 %collective-permute-done.4 = bf16[18,8,768]{2,1,0:T(8,128)(2,1)S(1)} collective-permute-done((bf16[18,8,768]{2,1,0:T(8,128)(2,1)S(1)}, bf16[18,8,768]{2,1,0:T(8,128)(2,1)S(1)}, u32[]{:S(2)}, u32[]{:S(2)}) %collective-permute-start.4) | collective-permute-done | bytes 221216 | tf_op jit(solution)/shard_map/ppermute | solution.py:25
  22.8 4.3 %collective-permute-start.7 = (bf16[128,640]{1,0:T(8,128)(2,1)S(1)}, bf16[128,640]{1,0:T(8,128)(2,1)S(1)}, u32[]{:S(2)}, u32[]{:S(2)}) collective-permute-start(bf16[128,640]{1,0:T(8,128)(2,1)S(1)} %constant_dynamic-slice_fusion), channel_id=1, source_target_pairs={{0,12},{2,14},{4,8},{6,10},{8,4},{10,6},{12,0},{14,2},{1,13},{3,15... | collective-permute-start | bytes 491528 | tf_op jit(solution)/shard_map/ppermute | solution.py:25
  27.2 1.0 %collective-permute-start.5 = (bf16[18,8,768]{2,1,0:T(8,128)(2,1)S(1)}, bf16[18,8,768]{2,1,0:T(8,128)(2,1)S(1)}, u32[]{:S(2)}, u32[]{:S(2)}) collective-permute-start(bf16[18,8,768]{2,1,0:T(8,128)(2,1)S(1)} %collective-permute-done.4), channel_id=1, source_target_pairs={{0,2},{2,0},{4,6},{6,4},{8,10},{10,8},{12,14},{14,12},{1,3},{3,1},... | collective-permute-start | bytes 663560 | tf_op jit(solution)/shard_map/ppermute | solution.py:25
  28.2 3.0 %collective-permute-done.7.rest_8_ = bf16[128,640]{1,0:T(8,128)(2,1)S(1)} collective-permute-done((bf16[128,640]{1,0:T(8,128)(2,1)S(1)}, bf16[128,640]{1,0:T(8,128)(2,1)S(1)}, u32[]{:S(2)}, u32[]{:S(2)}) %collective-permute-start.7) | collective-permute-done | bytes 163872 | tf_op jit(solution)/shard_map/ppermute | solution.py:25
  31.1 0.0 collective-permute-done.6
  31.2 0.7 %collective-permute-start.8 = (bf16[128,640]{1,0:T(8,128)(2,1)S(1)}, bf16[128,640]{1,0:T(8,128)(2,1)S(1)}, u32[]{:S(2)}, u32[]{:S(2)}) collective-permute-start(bf16[128,640]{1,0:T(8,128)(2,1)S(1)} %collective-permute-done.7.rest_8_), channel_id=1, source_target_pairs={{0,4},{2,6},{4,0},{6,2},{8,12},{10,14},{12,8},{14,10},{1,5},{3,7},... | collective-permute-start | bytes 491528 | tf_op jit(solution)/shard_map/ppermute | solution.py:25
  31.8 0.9 %collective-permute-start.9 = (bf16[128,640]{1,0:T(8,128)(2,1)S(1)}, bf16[128,640]{1,0:T(8,128)(2,1)S(1)}, u32[]{:S(2)}, u32[]{:S(2)}) collective-permute-start(bf16[128,640]{1,0:T(8,128)(2,1)S(1)} %collective-permute-done.7.rest_8_), channel_id=1, source_target_pairs={{0,2},{2,0},{4,6},{6,4},{8,10},{10,8},{12,14},{14,12},{1,3},{3,1},... | collective-permute-start | bytes 491528 | tf_op jit(solution)/shard_map/ppermute | solution.py:25
  32.7 2.0 %collective-permute-start.13 = (bf16[256,640]{1,0:T(8,128)(2,1)S(1)}, bf16[256,640]{1,0:T(8,128)(2,1)S(1)}, u32[]{:S(2)}, u32[]{:S(2)}) collective-permute-start(bf16[256,640]{1,0:T(8,128)(2,1)S(1)} %pad_maximum_fusion.rest_6_), channel_id=1, source_target_pairs={{0,4},{2,6},{4,0},{6,2},{8,12},{10,14},{12,8},{14,10},{1,5},{3,7},... | collective-permute-start | bytes 983048 | tf_op jit(solution)/shard_map/ppermute | solution.py:25
  34.8 0.1 collective-permute-done.5
  34.9 0.0 copy-done.6
  34.9 0.0 copy-done.7
  34.9 0.0 copy-done.8
  34.9 0.0 copy-start.1
  34.9 0.0 copy-start.2
  34.9 0.0 copy-start.3
  34.9 0.0 copy-start.4
  34.9 0.0 copy-start.5
  34.9 2.6 %tower.1 = (f32[96,768]{1,0:T(8,128)S(1)}, f32[80,768]{1,0:T(8,128)S(1)}, f32[80,768]{1,0:T(8,128)S(1)}) custom-call(s32[128]{0:T(128)S(1)} %copy-done.7, s32[4,16]{1,0:T(4,128)S(1)} %bitcast.18, s32[16]{0:T(128)S(1)} %copy-done.8, bf16[16,768]{1,0:T(8,128)(2,1)S(1)} %constant_dynamic-slice_fusion.2.deltas, ...), custom_call_target="tpu_custom_call" | custom-call | flops 1000000000 | bytes 40000000 | tf_op jit(solution)/shard_map/tower/pallas_call | solution.py:361
  37.5 0.1 collective-permute-done.8.rest_10_
  37.6 0.0 collective-permute-start.10
  37.6 0.0 collective-permute-done.9.rest_9_
  37.6 0.5 %collective-permute-start.12 = (f32[80,768]{1,0:T(8,128)S(1)}, f32[80,768]{1,0:T(8,128)S(1)}, u32[]{:S(2)}, u32[]{:S(2)}) collective-permute-start(f32[80,768]{1,0:T(8,128)S(1)} %get-tuple-element.54.rest_2_), channel_id=1, source_target_pairs={{0,1},{1,0},{2,3},{3,2},{4,5},{5,4},{6,7},{7,6},{8,9},{9,8},{10,11... | collective-permute-start | bytes 737288 | tf_op jit(solution)/shard_map/ppermute | solution.py:391
  38.1 0.1 collective-permute-start.11
  38.2 1.2 %collective-permute-start.14 = (bf16[128,640]{1,0:T(8,128)(2,1)S(1)}, bf16[128,640]{1,0:T(8,128)(2,1)S(1)}, u32[]{:S(2)}, u32[]{:S(2)}) collective-permute-start(bf16[128,640]{1,0:T(8,128)(2,1)S(1)} %collective-permute-done.8.rest_10_), channel_id=1, source_target_pairs={{0,2},{2,0},{4,6},{6,4},{8,10},{10,8},{12,14},{14,12},{1,3},{3,1},... | collective-permute-start | bytes 491528 | tf_op jit(solution)/shard_map/ppermute | solution.py:25
  39.4 1.7 %collective-permute-done.13.rest_7_ = bf16[256,640]{1,0:T(8,128)(2,1)S(1)} collective-permute-done((bf16[256,640]{1,0:T(8,128)(2,1)S(1)}, bf16[256,640]{1,0:T(8,128)(2,1)S(1)}, u32[]{:S(2)}, u32[]{:S(2)}) %collective-permute-start.13) | collective-permute-done | bytes 327712 | tf_op jit(solution)/shard_map/ppermute | solution.py:25
  41.1 0.0 collective-permute-done.12.rest_5_
  41.1 0.0 collective-permute-done.11.rest_4_
  41.1 0.0 collective-permute-done.10.rest_3_
  41.1 0.0 copy-done.1
  41.1 0.0 copy-done.2
  41.1 0.0 copy-done.3
  41.2 0.0 copy-done.4
  41.2 0.0 copy-done.5
  41.2 2.8 %near.1 = (bf16[256,256]{1,0:T(8,128)(2,1)S(1)}, f32[4,256,128]{2,1,0:T(8,128)S(1)}, f32[2,256,256]{2,1,0:T(8,128)S(1)}) custom-call(s32[16]{0:T(128)S(1)} %copy-done.4, f32[2]{0:T(128)S(1)} %copy-done.5, f32[1,1536]{1,0:T(1,128)S(1)} %reshape.6.gain, bf16[1536,256]{1,0:T(8,128)(2,1)S(1)} %copy-done.2, bf16[1536,256]{1,0:T(8,128)(2,1)S(1)} %copy-done.3, ...), custom_call_target="tpu_custom_call" | custom-call | tf_op jit(solution)/shard_map/near/pallas_call | solution.py:397
  43.9 0.8 %collective-permute-done.14.rest_0_ = bf16[128,640]{1,0:T(8,128)(2,1)S(1)} collective-permute-done((bf16[128,640]{1,0:T(8,128)(2,1)S(1)}, bf16[128,640]{1,0:T(8,128)(2,1)S(1)}, u32[]{:S(2)}, u32[]{:S(2)}) %collective-permute-start.14) | collective-permute-done | bytes 163872 | tf_op jit(solution)/shard_map/ppermute | solution.py:25
  44.7 1.8 %far.1 = bf16[256,384]{1,0:T(8,128)(2,1)} custom-call(s32[16]{0:T(128)S(1)} %copy-done.4, f32[2]{0:T(128)S(1)} %copy-done.5, bf16[256,256]{1,0:T(8,128)(2,1)S(1)} %get-tuple-element.58.queries, f32[4,256,128]{2,1,0:T(8,128)S(1)} %get-tuple-element.59.stats, f32[2,256,256]{2,1,0:T(8,128)S(1)} %get-tuple-element.60.sums, ...), custom_call_target="tpu_custom_call" | custom-call | tf_op jit(solution)/shard_map/far/pallas_call | solution.py:419
  (6 shorter events, 0.1 us)
Async XLA Ops:
  0.0 1.0 %copy-start = (bf16[16,8,1536]{2,1,0:T(8,128)(2,1)S(1)}, bf16[16,8,1536]{2,1,0:T(8,128)(2,1)}, u32[]{:S(2)}) copy-start(bf16[16,8,1536]{2,1,0:T(8,128)(2,1)} %param.15) | copy-start | bytes 1179652
  0.0 12.5 %copy-start.10 = (bf16[16,1536]{1,0:T(8,128)(2,1)S(1)}, bf16[16,1536]{1,0:T(8,128)(2,1)}, u32[]{:S(2)}) copy-start(bf16[16,1536]{1,0:T(8,128)(2,1)} %param.21) | copy-start | bytes 147460
  0.0 12.5 %copy-start.11 = (f32[1536]{0:T(1024)S(1)}, f32[1536]{0:T(1024)}, u32[]{:S(2)}) copy-start(f32[1536]{0:T(1024)} %param.23) | copy-start | bytes 18436
  0.0 12.5 %copy-start.9 = (bf16[17,1536]{1,0:T(8,128)(2,1)S(1)}, bf16[17,1536]{1,0:T(8,128)(2,1)}, u32[]{:S(2)}) copy-start(bf16[17,1536]{1,0:T(8,128)(2,1)} %param.22) | copy-start | bytes 156676
  0.0 34.9 %copy-start.6 = (s32[16,4]{0,1:T(4,128)S(1)}, s32[16,4]{0,1:T(4,128)}, u32[]{:S(2)}) copy-start(s32[16,4]{0,1:T(4,128)} %param.18) | copy-start | bytes 772
  0.0 34.9 %copy-start.7 = (s32[128]{0:T(128)S(1)}, s32[128]{0:T(128)}, u32[]{:S(2)}) copy-start(s32[128]{0:T(128)} %block_slot.1) | copy-start | bytes 1540
  0.0 34.8 %copy-start.8 = (s32[16]{0:T(128)S(1)}, s32[16]{0:T(128)}, u32[]{:S(2)}) copy-start(s32[16]{0:T(128)} %window_offsets.1) | copy-start | bytes 196
  1.1 8.9 %collective-permute-start.1 = (bf16[18,8,768]{2,1,0:T(8,128)(2,1)S(1)}, bf16[18,8,768]{2,1,0:T(8,128)(2,1)S(1)}, u32[]{:S(2)}, u32[]{:S(2)}) collective-permute-start(bf16[18,8,768]{2,1,0:T(8,128)(2,1)S(1)} %pack.1), channel_id=1, source_target_pairs={{0,4},{2,6},{4,0},{6,2},{8,12},{10,14},{12,8},{14,10},{1,5},{3,7},... | collective-permute-start | bytes 663560 | tf_op jit(solution)/shard_map/ppermute | solution.py:25
  4.1 6.9 %collective-permute-start.2 = (bf16[18,8,768]{2,1,0:T(8,128)(2,1)S(1)}, bf16[18,8,768]{2,1,0:T(8,128)(2,1)S(1)}, u32[]{:S(2)}, u32[]{:S(2)}) collective-permute-start(bf16[18,8,768]{2,1,0:T(8,128)(2,1)S(1)} %pack.1), channel_id=1, source_target_pairs={{0,2},{2,0},{4,6},{6,4},{8,10},{10,8},{12,14},{14,12},{1,3},{3,1},... | collective-permute-start | bytes 663560 | tf_op jit(solution)/shard_map/ppermute | solution.py:25
  5.6 11.0 %collective-permute-start = (bf16[18,8,768]{2,1,0:T(8,128)(2,1)S(1)}, bf16[18,8,768]{2,1,0:T(8,128)(2,1)S(1)}, u32[]{:S(2)}, u32[]{:S(2)}) collective-permute-start(bf16[18,8,768]{2,1,0:T(8,128)(2,1)S(1)} %pack.1), channel_id=1, source_target_pairs={{0,12},{2,14},{4,8},{6,10},{8,4},{10,6},{12,0},{14,2},{1,13},{3,15... | collective-permute-start | bytes 663560 | tf_op jit(solution)/shard_map/ppermute | solution.py:25
  11.0 7.4 %collective-permute-start.3 = (bf16[18,8,768]{2,1,0:T(8,128)(2,1)S(1)}, bf16[18,8,768]{2,1,0:T(8,128)(2,1)S(1)}, u32[]{:S(2)}, u32[]{:S(2)}) collective-permute-start(bf16[18,8,768]{2,1,0:T(8,128)(2,1)S(1)} %collective-permute-done.1), channel_id=1, source_target_pairs={{0,2},{2,0},{4,6},{6,4},{8,10},{10,8},{12,14},{14,12},{1,3},{3,1},... | collective-permute-start | bytes 663560 | tf_op jit(solution)/shard_map/ppermute | solution.py:25
  16.6 6.2 %collective-permute-start.4 = (bf16[18,8,768]{2,1,0:T(8,128)(2,1)S(1)}, bf16[18,8,768]{2,1,0:T(8,128)(2,1)S(1)}, u32[]{:S(2)}, u32[]{:S(2)}) collective-permute-start(bf16[18,8,768]{2,1,0:T(8,128)(2,1)S(1)} %collective-permute-done), channel_id=1, source_target_pairs={{0,4},{2,6},{4,0},{6,2},{8,12},{10,14},{12,8},{14,10},{1,5},{3,7},... | collective-permute-start | bytes 663560 | tf_op jit(solution)/shard_map/ppermute | solution.py:25
  18.4 12.8 %collective-permute-start.6 = (bf16[18,8,768]{2,1,0:T(8,128)(2,1)S(1)}, bf16[18,8,768]{2,1,0:T(8,128)(2,1)S(1)}, u32[]{:S(2)}, u32[]{:S(2)}) collective-permute-start(bf16[18,8,768]{2,1,0:T(8,128)(2,1)S(1)} %collective-permute-done), channel_id=1, source_target_pairs={{0,2},{2,0},{4,6},{6,4},{8,10},{10,8},{12,14},{14,12},{1,3},{3,1},... | collective-permute-start | bytes 663560 | tf_op jit(solution)/shard_map/ppermute | solution.py:25
  22.8 8.3 %collective-permute-start.7 = (bf16[128,640]{1,0:T(8,128)(2,1)S(1)}, bf16[128,640]{1,0:T(8,128)(2,1)S(1)}, u32[]{:S(2)}, u32[]{:S(2)}) collective-permute-start(bf16[128,640]{1,0:T(8,128)(2,1)S(1)} %constant_dynamic-slice_fusion), channel_id=1, source_target_pairs={{0,12},{2,14},{4,8},{6,10},{8,4},{10,6},{12,0},{14,2},{1,13},{3,15... | collective-permute-start | bytes 491528 | tf_op jit(solution)/shard_map/ppermute | solution.py:25
  27.2 7.7 %collective-permute-start.5 = (bf16[18,8,768]{2,1,0:T(8,128)(2,1)S(1)}, bf16[18,8,768]{2,1,0:T(8,128)(2,1)S(1)}, u32[]{:S(2)}, u32[]{:S(2)}) collective-permute-start(bf16[18,8,768]{2,1,0:T(8,128)(2,1)S(1)} %collective-permute-done.4), channel_id=1, source_target_pairs={{0,2},{2,0},{4,6},{6,4},{8,10},{10,8},{12,14},{14,12},{1,3},{3,1},... | collective-permute-start | bytes 663560 | tf_op jit(solution)/shard_map/ppermute | solution.py:25
  31.2 6.5 %collective-permute-start.8 = (bf16[128,640]{1,0:T(8,128)(2,1)S(1)}, bf16[128,640]{1,0:T(8,128)(2,1)S(1)}, u32[]{:S(2)}, u32[]{:S(2)}) collective-permute-start(bf16[128,640]{1,0:T(8,128)(2,1)S(1)} %collective-permute-done.7.rest_8_), channel_id=1, source_target_pairs={{0,4},{2,6},{4,0},{6,2},{8,12},{10,14},{12,8},{14,10},{1,5},{3,7},... | collective-permute-start | bytes 491528 | tf_op jit(solution)/shard_map/ppermute | solution.py:25
  31.8 5.8 %collective-permute-start.9 = (bf16[128,640]{1,0:T(8,128)(2,1)S(1)}, bf16[128,640]{1,0:T(8,128)(2,1)S(1)}, u32[]{:S(2)}, u32[]{:S(2)}) collective-permute-start(bf16[128,640]{1,0:T(8,128)(2,1)S(1)} %collective-permute-done.7.rest_8_), channel_id=1, source_target_pairs={{0,2},{2,0},{4,6},{6,4},{8,10},{10,8},{12,14},{14,12},{1,3},{3,1},... | collective-permute-start | bytes 491528 | tf_op jit(solution)/shard_map/ppermute | solution.py:25
  32.7 8.4 %collective-permute-start.13 = (bf16[256,640]{1,0:T(8,128)(2,1)S(1)}, bf16[256,640]{1,0:T(8,128)(2,1)S(1)}, u32[]{:S(2)}, u32[]{:S(2)}) collective-permute-start(bf16[256,640]{1,0:T(8,128)(2,1)S(1)} %pad_maximum_fusion.rest_6_), channel_id=1, source_target_pairs={{0,4},{2,6},{4,0},{6,2},{8,12},{10,14},{12,8},{14,10},{1,5},{3,7},... | collective-permute-start | bytes 983048 | tf_op jit(solution)/shard_map/ppermute | solution.py:25
  34.9 6.2 %copy-start.1 = (bf16[1536,384]{1,0:T(8,128)(2,1)S(1)}, bf16[1536,384]{1,0:T(8,128)(2,1)}, u32[]{:S(2)}) copy-start(bf16[1536,384]{1,0:T(8,128)(2,1)} %w_value.1) | copy-start | bytes 3538948
  34.9 6.2 %copy-start.2 = (bf16[1536,256]{1,0:T(8,128)(2,1)S(1)}, bf16[1536,256]{1,0:T(8,128)(2,1)}, u32[]{:S(2)}) copy-start(bf16[1536,256]{1,0:T(8,128)(2,1)} %w_query.1) | copy-start | bytes 2359300
  34.9 6.2 %copy-start.3 = (bf16[1536,256]{1,0:T(8,128)(2,1)S(1)}, bf16[1536,256]{1,0:T(8,128)(2,1)}, u32[]{:S(2)}) copy-start(bf16[1536,256]{1,0:T(8,128)(2,1)} %w_key.1) | copy-start | bytes 2359300
  34.9 6.2 %copy-start.4 = (s32[16]{0:T(128)S(1)}, s32[16]{0:T(128)}, u32[]{:S(2)}) copy-start(s32[16]{0:T(128)} %positions.3) | copy-start | bytes 196
  34.9 6.2 %copy-start.5 = (f32[2]{0:T(128)S(1)}, f32[2]{0:T(128)}, u32[]{:S(2)}) copy-start(f32[2]{0:T(128)} %slopes.3) | copy-start | bytes 28
  37.6 3.5 %collective-permute-start.10 = (f32[96,768]{1,0:T(8,128)S(1)}, f32[96,768]{1,0:T(8,128)S(1)}, u32[]{:S(2)}, u32[]{:S(2)}) collective-permute-start(f32[96,768]{1,0:T(8,128)S(1)} %get-tuple-element.51.rest_0_), channel_id=1, source_target_pairs={{0,1},{1,0},{2,3},{3,2},{4,5},{5,4},{6,7},{7,6},{8,9},{9,8},{10,11... | collective-permute-start | bytes 884744 | tf_op jit(solution)/shard_map/ppermute | solution.py:391
  37.6 3.5 %collective-permute-start.12 = (f32[80,768]{1,0:T(8,128)S(1)}, f32[80,768]{1,0:T(8,128)S(1)}, u32[]{:S(2)}, u32[]{:S(2)}) collective-permute-start(f32[80,768]{1,0:T(8,128)S(1)} %get-tuple-element.54.rest_2_), channel_id=1, source_target_pairs={{0,1},{1,0},{2,3},{3,2},{4,5},{5,4},{6,7},{7,6},{8,9},{9,8},{10,11... | collective-permute-start | bytes 737288 | tf_op jit(solution)/shard_map/ppermute | solution.py:391
  38.1 3.0 %collective-permute-start.11 = (f32[80,768]{1,0:T(8,128)S(1)}, f32[80,768]{1,0:T(8,128)S(1)}, u32[]{:S(2)}, u32[]{:S(2)}) collective-permute-start(f32[80,768]{1,0:T(8,128)S(1)} %get-tuple-element.52.rest_1_), channel_id=1, source_target_pairs={{0,1},{1,0},{2,3},{3,2},{4,5},{5,4},{6,7},{7,6},{8,9},{9,8},{10,11... | collective-permute-start | bytes 737288 | tf_op jit(solution)/shard_map/ppermute | solution.py:391
  38.2 6.5 %collective-permute-start.14 = (bf16[128,640]{1,0:T(8,128)(2,1)S(1)}, bf16[128,640]{1,0:T(8,128)(2,1)S(1)}, u32[]{:S(2)}, u32[]{:S(2)}) collective-permute-start(bf16[128,640]{1,0:T(8,128)(2,1)S(1)} %collective-permute-done.8.rest_10_), channel_id=1, source_target_pairs={{0,2},{2,0},{4,6},{6,4},{8,10},{10,8},{12,14},{14,12},{1,3},{3,1},... | collective-permute-start | bytes 491528 | tf_op jit(solution)/shard_map/ppermute | solution.py:25
